TPU v7x, 32 devices: a whole 2x2x4 slice. The times are simulated.
32 devices in a mesh: dp: 16 (over z, y, x), head: 2 (over core).
Axes of the slice: x: 2, y: 2, z: 4, core: 2. Of those that a mesh axis runs over, the one named last changes fastest.
Arguments:
- frames: bfloat16 [2, 8192, 768], P(None, ('dp', 'head')), may hold values from -6 to 6
- text_states: bfloat16 [2, 16, 4, 256, 768], P(None, 'dp'), may hold values from -6 to 6
- cotangent: bfloat16 [2, 8192, 768], P(None, ('dp', 'head')), may hold values from -6 to 6
- item_lengths: int32 [2, 16, 4], P(None, 'dp'), may hold values from 0 to 512, as said below
- text_lengths: int32 [2, 16, 4], P(None, 'dp'), may hold values from 1 to 256, as said below
- timesteps: int32 [2, 16, 4], P(None, 'dp'), may hold values from 0 to 999
- w_qkv: bfloat16 [768, 2304], P(('dp', 'head')), may hold values from -0.21875 to 0.21875
- w_proj: bfloat16 [768, 768], P(('dp', 'head')), may hold values from -0.625 to 0.625
- w_query: bfloat16 [768, 768], P(('dp', 'head')), may hold values from -0.21875 to 0.21875
- w_cproj: bfloat16 [768, 768], P(('dp', 'head')), may hold values from -0.625 to 0.625
- w_ada: bfloat16 [768, 6912], P(('dp', 'head')), may hold values from -0.21875 to 0.21875
- b_ada: bfloat16 [6912], P(('dp', 'head')), may hold values from -3 to 3
- w_kv: bfloat16 [2, 768, 768], P(None, 'dp', 'head'), may hold values from -0.21875 to 0.21875
- w_up: bfloat16 [768, 3072], P('dp', 'head'), may hold values from -0.21875 to 0.21875
- w_down: bfloat16 [3072, 768], P('head', 'dp'), may hold values from -0.109375 to 0.109375
Outputs:
- block_out: float32 [2, 8192, 768], P(None, ('dp', 'head'))
- frames_grad: float32 [2, 8192, 768], P(None, ('dp', 'head'))
- text_grad: float32 [2, 16, 4, 256, 768], P(None, 'dp', None, 'head')
- qkv_grad: float32 [768, 2304], P(('dp', 'head'))
- proj_grad: float32 [768, 768], P(('dp', 'head'))
- query_grad: float32 [768, 768], P(('dp', 'head'))
- cproj_grad: float32 [768, 768], P(('dp', 'head'))
- ada_grad: float32 [768, 6912], P(('dp', 'head'))
- ada_bias_grad: float32 [6912], P(('dp', 'head'))
- kv_grad: float32 [2, 768, 768], P(None, 'dp', 'head')
- up_grad: float32 [768, 3072], P('dp', 'head')
- down_grad: float32 [3072, 768], P('head', 'dp')
Inputs may be any that keep to these rules, and one draw needn't show every extreme that they name: `item_lengths`: A slab holds 4, 2 or 1 items of nominal length 128, 256 or 512 in its first slots, the other slots 0; an item's length lies between half its nominal length and that length, the first item of a slab has its nominal length, and every index of dp holds a single item of nominal length 512 in some micro-batch. `text_lengths`: the first slot of every slab has 256 live rows.
All inputs are finite; a program needn't handle non-finite values.
Results may differ from a plain program's by a relative error of at most 0.02.
Values may be sent and summed in bfloat16 or wider, within the bound.
No kernel may reach another device: no remote copies, remote signals or barrier semaphores. Data moves between devices by JAX's collectives and lax.ppermute only.
A program may use at most 256 MiB of HBM per device.

v0:
```python
import math

import jax
import jax.numpy as jnp
from jax import lax
from jax.sharding import PartitionSpec as P

HEADS = 12
DH = 64
TXT = 256
ITEMS = 4
SLAB = 512


PRECISE = lax.Precision.HIGHEST


def layer_norm(values):
    center = values - jnp.mean(values, axis=-1, keepdims=True)
    spread = jnp.mean(center * center, axis=-1, keepdims=True)
    return center * lax.rsqrt(spread + 1e-06)


def modulate(values, shift_by, scale_by):
    return layer_norm(values) * (1.0 + scale_by) + shift_by


def gelu_tanh(values):
    return jax.nn.gelu(values, approximate=True)


def time_embed(timesteps, width):
    halfwidth = width // 2
    frequency = jnp.exp(-math.log(10000.0) * jnp.arange(halfwidth).astype(jnp.float32) / halfwidth)
    angles = timesteps.astype(jnp.float32)[:, None] * frequency[None, :]
    return jnp.concatenate([jnp.cos(angles), jnp.sin(angles)], axis=-1)


def slab_layout(lengths):
    item_count = jnp.sum((lengths > 0).astype(jnp.int32))
    nominal = SLAB // item_count
    position = jnp.arange(SLAB, dtype=jnp.int32)
    item_slot = position // nominal
    one_hot = item_slot[:, None] == jnp.arange(ITEMS, dtype=jnp.int32)[None, :]
    own_length = jnp.sum(jnp.where(one_hot, lengths[None, :], 0), axis=1)
    frame_live = position - item_slot * nominal < own_length
    return (item_slot, one_hot.astype(jnp.float32), frame_live)


def text_layout(text_lengths):
    position = jnp.arange(ITEMS * TXT, dtype=jnp.int32)
    text_slot = position // TXT
    one_hot = text_slot[:, None] == jnp.arange(ITEMS, dtype=jnp.int32)[None, :]
    own_length = jnp.sum(jnp.where(one_hot, text_lengths[None, :], 0), axis=1)
    return (text_slot, position % TXT < own_length)


def matmul(left, right):
    return jnp.dot(left, right, preferred_element_type=jnp.float32)


def transposed_left(left, right):
    return lax.dot_general(
        left, right, (((0,), (0,)), ((), ())), preferred_element_type=jnp.float32
    )


def transposed_right(left, right):
    return lax.dot_general(
        left, right, (((1,), (1,)), ((), ())), preferred_element_type=jnp.float32
    )


def masked_scores(query_block, key_heads, query_slot, key_slot, key_live):
    allowed = (query_slot[:, None] == key_slot[None, :]) & key_live[None, :]
    scores = jnp.einsum(
        "qhd,khd->hqk", query_block, key_heads, preferred_element_type=jnp.float32
    ) * DH ** (-0.5)
    return jnp.where(allowed[None], scores, -1e30)


def attend(queries, keys, values, query_slot, key_slot, key_live, heads):
    row_count = queries.shape[0]
    block_rows = min(512, row_count)
    key_heads = keys.reshape(keys.shape[0], heads, DH)
    value_heads = values.reshape(values.shape[0], heads, DH)
    query_block = queries.reshape(block_rows, heads, DH)
    scores = masked_scores(query_block, key_heads, query_slot, key_slot, key_live)
    highest = jnp.max(scores, axis=-1, keepdims=True)
    exponent = jnp.exp(scores - highest)
    summed = jnp.sum(exponent, axis=-1, keepdims=True)
    weights = (exponent / summed).astype(jnp.bfloat16)
    output = jnp.einsum("hqk,khd->qhd", weights, value_heads, preferred_element_type=jnp.float32)
    outputs = output.reshape(block_rows, heads * DH)
    totals = highest + jnp.log(summed)
    return (outputs, totals)


def attend_back(queries, keys, values, grad_out, totals, query_slot, key_slot, key_live, heads):
    row_count = queries.shape[0]
    block_rows = min(512, row_count)
    score_scale = DH ** (-0.5)
    key_heads = keys.reshape(keys.shape[0], heads, DH)
    value_heads = values.reshape(values.shape[0], heads, DH)
    query_block = queries.reshape(block_rows, heads, DH)
    scores = masked_scores(query_block, key_heads, query_slot, key_slot, key_live)
    weights = jnp.exp(scores - totals)
    grad_block = grad_out.reshape(block_rows, heads, DH)
    grad_weights = jnp.einsum(
        "qhd,khd->hqk", grad_block, value_heads, preferred_element_type=jnp.float32
    )
    inner = jnp.sum(weights * grad_weights, axis=-1, keepdims=True)
    grad_scores = (weights * (grad_weights - inner)).astype(jnp.bfloat16)
    value_grad = jnp.einsum(
        "hqk,qhd->khd", weights.astype(jnp.bfloat16), grad_block, preferred_element_type=jnp.float32
    )
    query_part = (
        jnp.einsum("hqk,khd->qhd", grad_scores, key_heads, preferred_element_type=jnp.float32)
        * score_scale
    )
    query_grads = query_part.reshape(block_rows, heads * DH)
    key_grad = (
        jnp.einsum("hqk,qhd->khd", grad_scores, query_block, preferred_element_type=jnp.float32)
        * score_scale
    )
    width_here = heads * DH
    return (
        query_grads,
        key_grad.reshape(key_heads.shape[0], width_here),
        value_grad.reshape(value_heads.shape[0], width_here),
    )


def per_device(
    frames,
    text_states,
    cotangent,
    item_lengths,
    text_lengths,
    timesteps,
    w_qkv,
    w_proj,
    w_query,
    w_cproj,
    w_ada,
    b_ada,
    w_kv,
    w_up,
    w_down,
):
    head_count = lax.axis_size("head")
    head_index = lax.axis_index("head")
    heads_here = HEADS // head_count
    micro_count, own_rows, width = frames.shape

    def to_heads(values):
        return lax.all_to_all(values, "head", split_axis=2, concat_axis=1, tiled=True)

    def to_frames(values):
        return lax.all_to_all(values, "head", split_axis=1, concat_axis=2, tiled=True)

    def chip_frames(values):
        return lax.all_gather(values, "head", axis=0, tiled=True)

    def chip_sum(values):
        return lax.psum_scatter(
            values.astype(jnp.bfloat16), "head", scatter_dimension=0, tiled=True
        ).astype(jnp.float32)

    outputs = []
    input_grads = []
    text_grads = []
    for micro_step in range(micro_count):
        fetch_shared = (
            lax.all_gather(w_qkv, ("dp", "head"), axis=0, tiled=True),
            lax.all_gather(w_proj, ("dp", "head"), axis=0, tiled=True),
            lax.all_gather(w_query, ("dp", "head"), axis=0, tiled=True),
            lax.all_gather(w_cproj, ("dp", "head"), axis=0, tiled=True),
            lax.all_gather(w_ada, ("dp", "head"), axis=0, tiled=True),
            lax.all_gather(b_ada, ("dp", "head"), axis=0, tiled=True),
        )
        fetch_per_head = (
            lax.all_gather(w_kv, "dp", axis=1, tiled=True),
            lax.all_gather(w_up, "dp", axis=0, tiled=True),
            lax.all_gather(w_down, "dp", axis=1, tiled=True),
        )
        qkv_full, proj_full, query_full, cproj_full, ada_full, ada_bias = fetch_shared
        kv_full, up_full, down_full = fetch_per_head
        residual = frames[micro_step].astype(jnp.float32)
        text_rows = text_states[micro_step, 0].reshape(ITEMS * TXT, width)
        frame_slot, frame_onehot, frame_live = slab_layout(item_lengths[micro_step, 0])
        own_onehot = lax.dynamic_slice_in_dim(frame_onehot, head_index * own_rows, own_rows, 0)
        text_slot, text_live = text_layout(text_lengths[micro_step, 0])
        embedding = jax.nn.silu(time_embed(timesteps[micro_step, 0], width))
        item_mods = jnp.dot(
            embedding, ada_full.astype(jnp.float32), precision=PRECISE
        ) + ada_bias.astype(jnp.float32)
        frame_mods = jnp.dot(own_onehot, item_mods, precision=PRECISE)
        (
            shift_one,
            scale_one,
            gate_one,
            shift_two,
            scale_two,
            gate_two,
            shift_three,
            scale_three,
            gate_three,
        ) = jnp.split(frame_mods, 9, axis=1)
        normed_one = modulate(residual, shift_one, scale_one).astype(jnp.bfloat16)
        qkv_weight = qkv_full.reshape(width, 3, width)
        projected = jnp.einsum(
            "fd,dke->kfe", normed_one, qkv_weight, preferred_element_type=jnp.float32
        ).astype(jnp.bfloat16)
        by_head = to_heads(projected)
        attended, self_totals = attend(
            by_head[0], by_head[1], by_head[2], frame_slot, frame_slot, frame_live, heads_here
        )
        attended_frames = to_frames(attended.astype(jnp.bfloat16)[None])[0]
        branch_one = matmul(attended_frames, proj_full)
        after_one = residual + gate_one * branch_one
        normed_two = modulate(after_one, shift_two, scale_two).astype(jnp.bfloat16)
        cross_query = to_heads(matmul(normed_two, query_full).astype(jnp.bfloat16)[None])[0]
        text_kv = jnp.einsum(
            "rd,kde->kre", text_rows, kv_full, preferred_element_type=jnp.float32
        ).astype(jnp.bfloat16)
        crossed, cross_totals = attend(
            cross_query, text_kv[0], text_kv[1], frame_slot, text_slot, text_live, heads_here
        )
        crossed_frames = to_frames(crossed.astype(jnp.bfloat16)[None])[0]
        branch_two = matmul(crossed_frames, cproj_full)
        after_two = after_one + gate_two * branch_two
        normed_three = modulate(after_two, shift_three, scale_three).astype(jnp.bfloat16)
        chip_normed = chip_frames(normed_three)
        hidden_up = matmul(chip_normed, up_full)
        activated = gelu_tanh(hidden_up).astype(jnp.bfloat16)
        branch_three = chip_sum(matmul(activated, down_full))
        outputs.append(after_two + gate_three * branch_three)
        grad_out = cotangent[micro_step].astype(jnp.float32)
        grad_gate_three = grad_out * branch_three
        grad_branch = chip_frames((grad_out * gate_three).astype(jnp.bfloat16))
        down_grad = transposed_left(activated, grad_branch)
        grad_active = transposed_right(grad_branch, down_full)
        gelu_pull = jax.vjp(gelu_tanh, hidden_up)[1]
        grad_hidden = gelu_pull(grad_active)[0].astype(jnp.bfloat16)
        up_grad = transposed_left(chip_normed, grad_hidden)
        grad_normed = chip_sum(transposed_right(grad_hidden, up_full))
        norm_pull = jax.vjp(modulate, after_two, shift_three, scale_three)[1]
        grad_after_two, grad_shift_three, grad_scale_three = norm_pull(grad_normed)
        grad_after_two = grad_out + grad_after_two
        grad_gate_two = grad_after_two * branch_two
        grad_branch = (grad_after_two * gate_two).astype(jnp.bfloat16)
        cproj_grad = transposed_left(crossed_frames, grad_branch)
        grad_crossed = to_heads(
            transposed_right(grad_branch, cproj_full).astype(jnp.bfloat16)[None]
        )[0]
        grad_query_heads, grad_text_keys, grad_text_values = attend_back(
            cross_query,
            text_kv[0],
            text_kv[1],
            grad_crossed,
            cross_totals,
            frame_slot,
            text_slot,
            text_live,
            heads_here,
        )
        grad_query = to_frames(grad_query_heads.astype(jnp.bfloat16)[None])[0]
        grad_kv = jnp.stack([grad_text_keys, grad_text_values]).astype(jnp.bfloat16)
        kv_grad = jnp.einsum("rd,kre->kde", text_rows, grad_kv, preferred_element_type=jnp.float32)
        text_part = jnp.einsum("kre,kde->rd", grad_kv, kv_full, preferred_element_type=jnp.float32)
        text_grads.append(
            lax.psum_scatter(
                text_part.reshape(ITEMS, TXT, width).astype(jnp.bfloat16),
                "head",
                scatter_dimension=1,
                tiled=True,
            ).astype(jnp.float32)
        )
        query_grad = transposed_left(normed_two, grad_query)
        norm_pull = jax.vjp(modulate, after_one, shift_two, scale_two)[1]
        grad_after_one, grad_shift_two, grad_scale_two = norm_pull(
            transposed_right(grad_query, query_full)
        )
        grad_after_one = grad_after_two + grad_after_one
        grad_gate_one = grad_after_one * branch_one
        grad_branch = (grad_after_one * gate_one).astype(jnp.bfloat16)
        proj_grad = transposed_left(attended_frames, grad_branch)
        grad_attended = to_heads(
            transposed_right(grad_branch, proj_full).astype(jnp.bfloat16)[None]
        )[0]
        grad_queries, grad_keys, grad_values = attend_back(
            by_head[0],
            by_head[1],
            by_head[2],
            grad_attended,
            self_totals,
            frame_slot,
            frame_slot,
            frame_live,
            heads_here,
        )
        grad_projected = to_frames(
            jnp.stack([grad_queries, grad_keys, grad_values]).astype(jnp.bfloat16)
        )
        qkv_grad = jnp.einsum(
            "fd,kfe->dke", normed_one, grad_projected, preferred_element_type=jnp.float32
        ).reshape(width, 3 * width)
        norm_pull = jax.vjp(modulate, residual, shift_one, scale_one)[1]
        grad_residual, grad_shift_one, grad_scale_one = norm_pull(
            jnp.einsum(
                "kfe,dke->fd", grad_projected, qkv_weight, preferred_element_type=jnp.float32
            )
        )
        input_grads.append(grad_after_one + grad_residual)
        grad_mods = jnp.concatenate(
            [
                grad_shift_one,
                grad_scale_one,
                grad_gate_one,
                grad_shift_two,
                grad_scale_two,
                grad_gate_two,
                grad_shift_three,
                grad_scale_three,
                grad_gate_three,
            ],
            axis=1,
        )
        item_grads = jnp.dot(own_onehot.T, grad_mods, precision=PRECISE)
        ada_grad = jnp.dot(embedding.T, item_grads, precision=PRECISE)
        bias_grad = jnp.sum(item_grads, axis=0)
        grads_now = (
            (qkv_grad, proj_grad, query_grad, cproj_grad, ada_grad, bias_grad),
            (kv_grad, up_grad, down_grad),
        )
        shared_grads = grads_now[0]
        head_grads = grads_now[1]
        shared = (
            lax.psum_scatter(shared_grads[0], ("dp", "head"), scatter_dimension=0, tiled=True),
            lax.psum_scatter(shared_grads[1], ("dp", "head"), scatter_dimension=0, tiled=True),
            lax.psum_scatter(shared_grads[2], ("dp", "head"), scatter_dimension=0, tiled=True),
            lax.psum_scatter(shared_grads[3], ("dp", "head"), scatter_dimension=0, tiled=True),
            lax.psum_scatter(shared_grads[4], ("dp", "head"), scatter_dimension=0, tiled=True),
            lax.psum_scatter(shared_grads[5], ("dp", "head"), scatter_dimension=0, tiled=True),
        )
        per_head = (
            lax.psum_scatter(head_grads[0], "dp", scatter_dimension=1, tiled=True),
            lax.psum_scatter(head_grads[1], "dp", scatter_dimension=0, tiled=True),
            lax.psum_scatter(head_grads[2], "dp", scatter_dimension=1, tiled=True),
        )
        grads_now = (shared, per_head)
        collected = (
            grads_now
            if micro_step == 0
            else jax.tree.map(lambda former, latter: former + latter, collected, grads_now)
        )
    (qkv_sum, proj_sum, query_sum, cproj_sum, ada_sum, bias_sum), (kv_sum, up_sum, down_sum) = (
        collected
    )
    return (
        jnp.stack(outputs),
        jnp.stack(input_grads),
        jnp.stack(text_grads)[:, None],
        qkv_sum,
        proj_sum,
        query_sum,
        cproj_sum,
        ada_sum,
        bias_sum,
        kv_sum,
        up_sum,
        down_sum,
    )


def solution(mesh):
    return jax.shard_map(
        per_device,
        mesh=mesh,
        in_specs=(
            P(None, ("dp", "head"), None),
            P(None, "dp", None, None, None),
            P(None, ("dp", "head"), None),
            P(None, "dp", None),
            P(None, "dp", None),
            P(None, "dp", None),
            P(("dp", "head"), None),
            P(("dp", "head"), None),
            P(("dp", "head"), None),
            P(("dp", "head"), None),
            P(("dp", "head"), None),
            P(("dp", "head")),
            P(None, "dp", "head"),
            P("dp", "head"),
            P("head", "dp"),
        ),
        out_specs=(
            P(None, ("dp", "head"), None),
            P(None, ("dp", "head"), None),
            P(None, "dp", None, "head", None),
            P(("dp", "head"), None),
            P(("dp", "head"), None),
            P(("dp", "head"), None),
            P(("dp", "head"), None),
            P(("dp", "head"), None),
            P(("dp", "head")),
            P(None, "dp", "head"),
            P("dp", "head"),
            P("head", "dp"),
        ),
        check_vma=False,
    )
```

profile of v0, /device:TPU:0, one launch (start us, length us, event | category | flops | bytes accessed | tf_op | source)
XLA Modules:
  0.0 1799.3 jit_solution(12229608226263224541)
XLA Ops:
  24.5 42.4 %all-reduce = bf16[6912]{0:T(1024)(128)(2,1)S(1)} all-reduce(bf16[6912]{0:T(1024)(128)(2,1)S(1)} %dynamic-update-slice), channel_id=1, replica_groups=mesh['dp'=16,'head'=2] {'dp','head'}, use_global_device_ids=true, to_apply=%add | all-reduce | flops 6912 | bytes 27648
  81.1 50.6 %all-gather.11.cloned.1.call-done = bf16[768,2304]{1,0:T(8,128)(2,1)} async-done(((bf16[24,2304]{1,0:T(8,128)(2,1)}), bf16[768,2304]{1,0:T(8,128)(2,1)}) %all-gather.11.cloned.1.call-update) | async-done | bytes 3538960 | tf_op jit(solution)/shard_map/all_gather | solution.py:175
  131.6 5.7 copy.258
  137.4 83.1 %all-gather.9.cloned.1.call-done = bf16[768,6912]{1,0:T(8,128)(2,1)} async-done(((bf16[24,6912]{1,0:T(8,128)(2,1)}), bf16[768,6912]{1,0:T(8,128)(2,1)}) %all-gather.9.cloned.1.call-update) | async-done | bytes 10616848 | tf_op jit(solution)/shard_map/all_gather | solution.py:179
  220.5 8.6 convolution_add_fusion.1
  248.8 5.4 all_to_all.246
  265.5 5.0 all_to_all.247
  313.8 17.7 all-gather.17.cloned.1.call-done
  335.1 4.8 reduce.4
  340.9 5.0 all_to_all.250
  356.9 4.8 reduce.6
  362.7 4.8 all_to_all.251
  386.4 4.8 reduce.7
  392.3 5.2 all_to_all.252
  444.5 6.9 all-gather.23.cloned.1.call-done
  451.4 5.0 fusion.182
  456.4 59.0 %all-gather.21.cloned.1.call-done = bf16[768,1536]{1,0:T(8,128)(2,1)} async-done(((bf16[48,1536]{1,0:T(8,128)(2,1)}), bf16[768,1536]{1,0:T(8,128)(2,1)}) %all-gather.21.cloned.1.call-update) | async-done | bytes 2359312 | tf_op jit(solution)/shard_map/all_gather | solution.py:184
  515.3 7.6 fusion.29
  537.7 5.4 convolution_convert_fusion.6
  543.3 5.6 convolution_convert_fusion.7
  560.2 8.4 reduce-scatter.14.cloned.1.call-done
  579.1 4.7 reduce.10
  585.7 5.9 all_to_all.254
  598.0 7.8 fusion.46
  605.8 8.8 multiply_reduce_fusion
  621.1 4.4 all_to_all.255
  626.7 6.8 fusion.43
  633.6 8.8 multiply_reduce_fusion.1
  647.1 9.4 multiply_convert_fusion
  660.2 9.4 multiply_convert_fusion.1
  680.0 5.3 copy.315
  689.8 4.4 bitcast_convert_fusion.1
  694.3 4.8 fusion.52
  712.3 4.9 fusion.49
  795.7 5.1 fusion.55
  803.9 4.6 multiply_reduce_fusion.3
  826.3 5.2 all_to_all.260
  837.1 4.7 multiply_reduce_fusion.2
  855.5 5.0 all_to_all.261
  895.0 17.1 fusion.155
  912.2 20.5 %convolution_add_fusion = f32[768,6912]{1,0:T(8,128)} fusion(f32[768,6912]{1,0:T(8,128)S(1)} %fusion.155, f32[4,6912]{1,0:T(4,128)S(1)} %get-tuple-element.204, f32[4,384]{1,0:T(4,128)S(1)} %copy-done.131, f32[4,384]{1,0:T(4,128)S(1)} %copy-done.133), kind=kOutput, calls=%fused_computation | convolution fusion | flops 260127744 | bytes 42590208 | tf_op jit(solution)/shard_map/dot_general | solution.py:331
  934.6 40.9 %all-reduce.1 = f32[6912]{0:T(1024)S(1)} all-reduce(f32[6912]{0:T(1024)S(1)} %add.405), channel_id=22, replica_groups=mesh['dp'=16,'head'=2] {'dp','head'}, use_global_device_ids=true, to_apply=%region_59.60.clone | all-reduce | flops 6912 | bytes 55296
  983.5 67.8 %reduce-scatter.28.cloned.1.call-done = f32[24,768]{1,0:T(8,128)} async-done(((f32[768,768]{1,0:T(8,128)}), f32[24,768]{1,0:T(8,128)}) %reduce-scatter.28.cloned.1.call-update) | async-done | bytes 73744 | tf_op jit(solution)/shard_map/reduce_scatter | solution.py:341
  1051.4 104.7 %reduce-scatter.30.cloned.1.call-done = f32[24,768]{1,0:T(8,128)} async-done(((f32[768,768]{1,0:T(8,128)}), f32[24,768]{1,0:T(8,128)}) %reduce-scatter.30.cloned.1.call-update) | async-done | bytes 73744 | tf_op jit(solution)/shard_map/reduce_scatter | solution.py:342
  1156.0 141.5 %reduce-scatter.36.cloned.1.call-done = f32[48,1536]{1,0:T(8,128)} async-done(((f32[768,1536]{1,0:T(8,128)}), f32[48,1536]{1,0:T(8,128)}) %reduce-scatter.36.cloned.1.call-update) | async-done | bytes 294928 | tf_op jit(solution)/shard_map/reduce_scatter | solution.py:349
  1297.5 143.0 %reduce-scatter.38.cloned.1.call-done = f32[1536,48]{0,1:T(8,128)} async-done(((f32[1536,768]{0,1:T(8,128)}), f32[1536,48]{0,1:T(8,128)}) %reduce-scatter.38.cloned.1.call-update) | async-done | bytes 294928 | tf_op jit(solution)/shard_map/reduce_scatter | solution.py:350
  1440.5 124.5 %reduce-scatter.26.cloned.1.call-done = f32[24,2304]{1,0:T(8,128)} async-done(((f32[768,2304]{1,0:T(8,128)}), f32[24,2304]{1,0:T(8,128)}) %reduce-scatter.26.cloned.1.call-update) | async-done | bytes 221200 | tf_op jit(solution)/shard_map/reduce_scatter | solution.py:340
  1565.0 227.2 %reduce-scatter.34.cloned.1.call-done = f32[24,6912]{1,0:T(8,128)} async-done(((f32[768,6912]{1,0:T(8,128)}), f32[24,6912]{1,0:T(8,128)}) %reduce-scatter.34.cloned.1.call-update) | async-done | bytes 663568 | tf_op jit(solution)/shard_map/reduce_scatter | solution.py:344
  (683 shorter events, 434.5 us)
Async XLA Ops:
  7.2 61.7 %copy-start.91 = (bf16[2,1,4,256,768]{4,3,2,1,0:T(8,128)(2,1)S(1)}, bf16[2,1,4,256,768]{4,3,2,1,0:T(8,128)(2,1)}, u32[]{:S(2)}) copy-start(bf16[2,1,4,256,768]{4,3,2,1,0:T(8,128)(2,1)} %param.16) | copy-start | bytes 9437188
  7.2 65.6 %all-gather.15.cloned.1.call-start = ((), (), s32[]{:S(2)}) async-start(), calls=%async_computation.32 | async-start | bytes 1253376 | tf_op jit(solution)/shard_map/all_gather | solution.py:183
  7.9 123.7 %all-gather.11.cloned.1.call-start = ((), (), s32[]{:S(2)}) async-start(), calls=%async_computation.30 | async-start | bytes 3649536 | tf_op jit(solution)/shard_map/all_gather | solution.py:175
  8.7 211.8 %all-gather.9.cloned.1.call-start = ((), (), s32[]{:S(2)}) async-start(), calls=%async_computation.29 | async-start | bytes 10948608 | tf_op jit(solution)/shard_map/all_gather | solution.py:179
  9.4 293.0 %all-gather.13.cloned.1.call-start = ((), (), s32[]{:S(2)}) async-start(), calls=%async_computation.31 | async-start | bytes 1216512 | tf_op jit(solution)/shard_map/all_gather | solution.py:176
  10.0 321.5 %all-gather.17.cloned.1.call-start = ((), (), s32[]{:S(2)}) async-start(), calls=%async_computation.33 | async-start | bytes 1216512 | tf_op jit(solution)/shard_map/all_gather | solution.py:177
  10.6 414.2 %all-gather.19.cloned.1.call-start = ((), (), s32[]{:S(2)}) async-start(), calls=%async_computation.34 | async-start | bytes 1216512 | tf_op jit(solution)/shard_map/all_gather | solution.py:178
  11.1 440.3 %all-gather.23.cloned.1.call-start = ((), (), s32[]{:S(2)}) async-start(), calls=%async_computation.36 | async-start | bytes 2506752 | tf_op jit(solution)/shard_map/all_gather | solution.py:185
  11.9 503.4 %all-gather.21.cloned.1.call-start = ((), (), s32[]{:S(2)}) async-start(), calls=%async_computation.35 | async-start | bytes 2506752 | tf_op jit(solution)/shard_map/all_gather | solution.py:184
  12.6 536.6 %reduce-scatter.20.cloned.1.call-start = ((), (), s32[]{:S(2)}) async-start(), calls=%async_computation.40 | async-start | bytes 1179648 | tf_op jit(solution)/shard_map/reduce_scatter | solution.py:166
  20.2 208.8 %copy-start.168 = (pred[512,4]{0,1:T(4,128)(4,1)}, pred[512,4]{0,1:T(4,128)(4,1)S(1)}, u32[]{:S(2)}) copy-start(pred[512,4]{0,1:T(4,128)(4,1)S(1)} %iota_compare_fusion.1) | copy-start | bytes 6148
  20.3 216.1 %copy-start.166 = (pred[512,4]{0,1:T(4,128)(4,1)}, pred[512,4]{0,1:T(4,128)(4,1)S(1)}, u32[]{:S(2)}) copy-start(pred[512,4]{0,1:T(4,128)(4,1)S(1)} %iota_compare_fusion.2) | copy-start | bytes 6148
  21.6 217.8 %copy-start.126 = (f32[256]{0:T(256)}, f32[256]{0:T(256)S(1)}, u32[]{:S(2)}) copy-start(f32[256]{0:T(256)S(1)} %get-tuple-element.205) | copy-start | bytes 3076
  21.6 217.8 %copy-start.128 = (f32[256]{0:T(256)}, f32[256]{0:T(256)S(1)}, u32[]{:S(2)}) copy-start(f32[256]{0:T(256)S(1)} %get-tuple-element.206) | copy-start | bytes 3076
  23.1 216.2 %copy-start.162 = (f32[256]{0:T(256)}, f32[256]{0:T(256)S(1)}, u32[]{:S(2)}) copy-start(f32[256]{0:T(256)S(1)} %fusion.139) | copy-start | bytes 3076
  23.2 216.2 %copy-start.164 = (f32[256]{0:T(256)}, f32[256]{0:T(256)S(1)}, u32[]{:S(2)}) copy-start(f32[256]{0:T(256)S(1)} %fusion.142) | copy-start | bytes 3076
  72.7 147.8 %copy-start.130 = (f32[4,384]{1,0:T(4,128)}, f32[4,384]{1,0:T(4,128)S(1)}, u32[]{:S(2)}) copy-start(f32[4,384]{1,0:T(4,128)S(1)} %get-tuple-element.165) | copy-start | bytes 18436
  72.7 147.7 %copy-start.132 = (f32[4,384]{1,0:T(4,128)}, f32[4,384]{1,0:T(4,128)S(1)}, u32[]{:S(2)}) copy-start(f32[4,384]{1,0:T(4,128)S(1)} %get-tuple-element.166) | copy-start | bytes 18436
  72.8 159.3 %copy-start.134 = (f32[4,384]{1,0:T(4,128)}, f32[4,384]{1,0:T(4,128)S(1)}, u32[]{:S(2)}) copy-start(f32[4,384]{1,0:T(4,128)S(1)} %get-tuple-element.161) | copy-start | bytes 18436
  72.8 159.3 %copy-start.136 = (f32[4,384]{1,0:T(4,128)}, f32[4,384]{1,0:T(4,128)S(1)}, u32[]{:S(2)}) copy-start(f32[4,384]{1,0:T(4,128)S(1)} %get-tuple-element.162) | copy-start | bytes 18436
  256.7 31.7 %copy-start.64 = (bf16[512,6,64]{0,2,1:T(8,128)(2,1)}, bf16[512,6,64]{0,2,1:T(8,128)(2,1)S(1)}, u32[]{:S(2)}) copy-start(bf16[512,6,64]{0,2,1:T(8,128)(2,1)S(1)} %reshape_squeeze.68) | copy-start | bytes 1179652
  307.6 427.8 %copy-start.9 = (f32[256,768]{1,0:T(8,128)}, f32[256,768]{1,0:T(8,128)S(1)}, u32[]{:S(2)}) copy-start(f32[256,768]{1,0:T(8,128)S(1)} %get-tuple-element.156) | copy-start | bytes 2359300
  313.8 21.2 %copy-start.81 = (bf16[256,768]{1,0:T(8,128)(2,1)}, bf16[256,768]{1,0:T(8,128)(2,1)S(1)}, u32[]{:S(2)}) copy-start(bf16[256,768]{1,0:T(8,128)(2,1)S(1)} %fusion.109) | copy-start | bytes 1179652
  351.6 51.1 %copy-start.54 = (bf16[512,6,64]{0,2,1:T(8,128)(2,1)}, bf16[512,6,64]{0,2,1:T(8,128)(2,1)S(1)}, u32[]{:S(2)}) copy-start(bf16[512,6,64]{0,2,1:T(8,128)(2,1)S(1)} %reshape_squeeze.78) | copy-start | bytes 1179652
  402.6 22.2 %copy-start.70 = (bf16[1,256,2,384]{1,3,2,0:T(8,128)(2,1)}, bf16[1,256,2,384]{1,3,2,0:T(8,128)(2,1)S(1)}, u32[]{:S(2)}) copy-start(bf16[1,256,2,384]{1,3,2,0:T(8,128)(2,1)S(1)} %copy.268) | copy-start | bytes 1179652
  427.9 140.7 %copy-start.13 = (f32[256,768]{1,0:T(8,128)}, f32[256,768]{1,0:T(8,128)S(1)}, u32[]{:S(2)}) copy-start(f32[256,768]{1,0:T(8,128)S(1)} %get-tuple-element.111) | copy-start | bytes 2359300
  427.9 140.7 %copy-start.142 = (f32[256]{0:T(256)}, f32[256]{0:T(256)S(1)}, u32[]{:S(2)}) copy-start(f32[256]{0:T(256)S(1)} %broadcast_multiply_fusion.3) | copy-start | bytes 3076
  430.9 126.0 %copy-start.144 = (f32[256]{0:T(256)}, f32[256]{0:T(256)S(1)}, u32[]{:S(2)}) copy-start(f32[256]{0:T(256)S(1)} %broadcast_multiply_fusion) | copy-start | bytes 3076
  431.2 137.4 %copy-start.150 = (f32[256]{0:T(256)}, f32[256]{0:T(256)S(1)}, u32[]{:S(2)}) copy-start(f32[256]{0:T(256)S(1)} %fusion.141) | copy-start | bytes 3076
  431.2 125.7 %copy-start.152 = (f32[256]{0:T(256)}, f32[256]{0:T(256)S(1)}, u32[]{:S(2)}) copy-start(f32[256]{0:T(256)S(1)} %fusion.144) | copy-start | bytes 3076
  526.4 24.6 %reduce-scatter.18.cloned.1.call-start = ((), (), s32[]{:S(2)}) async-start(), calls=%async_computation.39 | async-start | bytes 1179648 | tf_op jit(solution)/shard_map/reduce_scatter | solution.py:166
  537.7 19.2 %reduce-scatter.16.cloned.1.call-start = ((), (), s32[]{:S(2)}) async-start(), calls=%async_computation.38 | async-start | bytes 1179648 | tf_op jit(solution)/shard_map/reduce_scatter | solution.py:166
  543.2 25.3 %reduce-scatter.14.cloned.1.call-start = ((), (), s32[]{:S(2)}) async-start(), calls=%async_computation.37 | async-start | bytes 1179648 | tf_op jit(solution)/shard_map/reduce_scatter | solution.py:166
  548.9 429.7 %all-reduce.5.cloned.1.call-start = ((), (), s32[]{:S(2)}) async-start(), calls=%async_computation.50 | async-start | bytes 4718592
  551.0 17.5 copy-start.48
  574.2 40.4 %copy-start.73 = (bf16[256,768]{1,0:T(8,128)(2,1)}, bf16[256,768]{1,0:T(8,128)(2,1)S(1)}, u32[]{:S(2)}) copy-start(bf16[256,768]{1,0:T(8,128)(2,1)S(1)} %get-tuple-element.151) | copy-start | bytes 1179652
  685.3 295.0 %reduce-scatter.24.cloned.1.call-start = ((), (), s32[]{:S(2)}) async-start(), calls=%async_computation.42 | async-start | bytes 2359296 | tf_op jit(solution)/shard_map/reduce_scatter | solution.py:273
  689.7 290.6 %reduce-scatter.22.cloned.1.call-start = ((), (), s32[]{:S(2)}) async-start(), calls=%async_computation.41 | async-start | bytes 2359296 | tf_op jit(solution)/shard_map/reduce_scatter | solution.py:273
  694.2 289.3 %reduce-scatter.32.cloned.1.call-start = ((), (), s32[]{:S(2)}) async-start(), calls=%async_computation.46 | async-start | bytes 2433024 | tf_op jit(solution)/shard_map/reduce_scatter | solution.py:343
  733.2 318.2 %reduce-scatter.28.cloned.1.call-start = ((), (), s32[]{:S(2)}) async-start(), calls=%async_computation.44 | async-start | bytes 2433024 | tf_op jit(solution)/shard_map/reduce_scatter | solution.py:341
  747.9 408.2 %reduce-scatter.30.cloned.1.call-start = ((), (), s32[]{:S(2)}) async-start(), calls=%async_computation.45 | async-start | bytes 2433024 | tf_op jit(solution)/shard_map/reduce_scatter | solution.py:342
  750.9 546.6 %reduce-scatter.36.cloned.1.call-start = ((), (), s32[]{:S(2)}) async-start(), calls=%async_computation.48 | async-start | bytes 5013504 | tf_op jit(solution)/shard_map/reduce_scatter | solution.py:349
  757.9 682.6 %reduce-scatter.38.cloned.1.call-start = ((), (), s32[]{:S(2)}) async-start(), calls=%async_computation.49 | async-start | bytes 5013504 | tf_op jit(solution)/shard_map/reduce_scatter | solution.py:350
  765.7 799.3 %reduce-scatter.26.cloned.1.call-start = ((), (), s32[]{:S(2)}) async-start(), calls=%async_computation.43 | async-start | bytes 7299072 | tf_op jit(solution)/shard_map/reduce_scatter | solution.py:340
  874.3 917.9 %reduce-scatter.34.cloned.1.call-start = ((), (), s32[]{:S(2)}) async-start(), calls=%async_computation.47 | async-start | bytes 21897216 | tf_op jit(solution)/shard_map/reduce_scatter | solution.py:344
  895.0 17.2 copy-start.131
  932.7 43.5 %copy-start.98 = (f32[1,256,768]{2,1,0:T(8,128)S(1)}, f32[1,256,768]{2,1,0:T(8,128)}, u32[]{:S(2)}) copy-start(f32[1,256,768]{2,1,0:T(8,128)} %get-tuple-element.119) | copy-start | bytes 2359300
  932.7 43.5 %copy-start.99 = (f32[1,256,768]{2,1,0:T(8,128)S(1)}, f32[1,256,768]{2,1,0:T(8,128)}, u32[]{:S(2)}) copy-start(f32[1,256,768]{2,1,0:T(8,128)} %get-tuple-element.118) | copy-start | bytes 2359300
  (152 other events, 574.1 us)
Sparse Core Ops, SparseCore 0:
  10.7 59.0 all-gather.14
  72.7 58.8 all-gather.10
  134.5 85.9 all-gather.8
  223.2 52.4 all-gather.12
  278.5 52.9 all-gather.16
  334.3 52.9 all-gather.18
  390.1 61.2 all-gather.22
  454.2 61.0 all-gather.20
  526.5 7.0 reduce-scatter.19
  537.8 7.3 reduce-scatter.17
  547.5 9.3 reduce-scatter.15
  559.1 9.3 reduce-scatter.13
  685.4 132.1 all-reduce.4
  819.8 8.5 reduce-scatter.23
  830.5 10.2 reduce-scatter.21
  847.4 100.2 reduce-scatter.31
  953.3 97.9 reduce-scatter.27
  1057.9 98.0 reduce-scatter.29
  1161.8 135.6 reduce-scatter.35
  1303.9 136.5 reduce-scatter.37
  1446.7 118.2 reduce-scatter.25
  1573.1 219.0 reduce-scatter.33
where the time goes:
time: 1810 us; the launch traced here: 1800 us
  waiting for transfers between devices  1040 us (57%)
  matrix products  272 us (15%)
  blocking collectives  168 us (9%)
  local copies, waits for them, and re-layouts  162 us (9%)
  other arithmetic  129 us (7%)
  between operations  22 us (1%)
    reduce_scatter x1, waiting for transfers between devices, per_device(): lax.psum_scatter(shared_grads[4], ('dp', 'head'), scatter_dimension=0, ti...  227 us
    reduce_scatter x1, waiting for transfers between devices, per_device(): lax.psum_scatter(head_grads[2], 'dp', scatter_dimension=1, tiled=True)  143 us
    reduce_scatter x1, waiting for transfers between devices, per_device(): lax.psum_scatter(head_grads[1], 'dp', scatter_dimension=0, tiled=True)  141 us
    reduce_scatter x1, waiting for transfers between devices, per_device(): lax.psum_scatter(shared_grads[0], ('dp', 'head'), scatter_dimension=0, ti...  125 us
    reduce_scatter x1, waiting for transfers between devices, per_device(): lax.psum_scatter(shared_grads[2], ('dp', 'head'), scatter_dimension=0, ti...  105 us
    unnamed x2, blocking collectives  83.4 us
    all_gather x1, waiting for transfers between devices, per_device(): lax.all_gather(w_ada, ('dp', 'head'), axis=0, tiled=True)  83.1 us
    reduce_scatter x1, waiting for transfers between devices, per_device(): lax.psum_scatter(shared_grads[1], ('dp', 'head'), scatter_dimension=0, ti...  67.8 us
  transfers between devices with their start and end apart: 22, of which 13 were waited for; matrix products, arithmetic and copies ran while one was open for 23% of the time, Pallas kernels for 0%

commit v1 on v0

v1 whole, which is shorter than its diff:
```python
import functools
import math

import jax
import jax.numpy as jnp
from jax import lax
from jax.experimental import pallas as pl
from jax.experimental.pallas import tpu as pltpu
from jax.sharding import PartitionSpec as P

HEADS = 12
DH = 64
TXT = 256
ITEMS = 4
SLAB = 512
BLOCKS = 4
ROWS = SLAB // BLOCKS
PAIR = 2 * DH
SCALE = DH**-0.5
MASKED = -1e30
PLANE = 16

BF16 = jnp.bfloat16
F32 = jnp.float32
PRECISE = lax.Precision.HIGHEST
BOTH = ("dp", "head")


def params(mebibytes):
    return pltpu.CompilerParams(vmem_limit_bytes=mebibytes * 2**20)


def cost(microseconds):
    return pl.CostEstimate(
        flops=int(1.1e9 * microseconds), bytes_accessed=int(3.5e6 * microseconds), transcendentals=0
    )


def mm(left, right):
    return jnp.dot(left, right, preferred_element_type=F32)


def mm_tl(left, right):
    return lax.dot_general(left, right, (((0,), (0,)), ((), ())), preferred_element_type=F32)


def mm_tr(left, right):
    return lax.dot_general(left, right, (((1,), (1,)), ((), ())), preferred_element_type=F32)


def swap_core(values):
    return lax.ppermute(values, "head", [(0, 1), (1, 0)])


def hop(values, first_core, second_core):
    steps = (first_core, second_core)
    pairs = [(2 * d + c, 2 * (d ^ steps[c]) + c) for d in range(PLANE) for c in range(2)]
    return lax.ppermute(values, BOTH, pairs)


def cut_kernel(groups, core, *refs):
    ins, (kept, sent) = refs[:-2], refs[-2:]
    start = 0
    for source, count in zip(ins, groups):
        half = source.shape[1] // count // 2
        for at in range(count):
            for side, out in ((core[0], kept), (1 - core[0], sent)):
                cols = pl.ds(pl.multiple_of((2 * at + side) * half, 128), half)
                out[:, start : start + half] = source[:, cols]
            start += half


def cut(core, shards, groups):
    rows = shards[0].shape[0]
    width = sum(shard.shape[1] for shard in shards) // 2
    held = pl.BlockSpec(memory_space=pltpu.VMEM)
    return pl.pallas_call(
        functools.partial(cut_kernel, groups),
        out_shape=[jax.ShapeDtypeStruct((rows, width), BF16)] * 2,
        in_specs=[pl.BlockSpec(memory_space=pltpu.SMEM)] + [held] * len(shards),
        out_specs=[held] * 2,
        compiler_params=params(8),
        cost_estimate=cost(1),
        name="cut",
    )(jnp.stack([core]).astype(jnp.int32), *shards)


def near_bits(core):
    return jnp.where(core == 0, 1, 2), jnp.where(core == 0, 2, 1)


def tie(value, *after):
    return lax.optimization_barrier((value,) + after)[0]


def place_kernel(starts, widths, dst, *refs):
    pieces, outs = refs[:4], refs[4:]
    for quarter in range(4):
        for step in range(4):
            at = dst[4 * quarter + step]
            for out, start, width in zip(outs, starts, widths):
                out[at] = pieces[quarter][step, :, start : start + width]


def place(dst, pieces, widths):
    _, rows, total = pieces[0].shape
    starts = [sum(widths[:i]) for i in range(len(widths))]
    held = pl.BlockSpec(memory_space=pltpu.VMEM)
    outs = pl.pallas_call(
        functools.partial(place_kernel, starts, widths),
        out_shape=[jax.ShapeDtypeStruct((PLANE, rows, width), BF16) for width in widths],
        in_specs=[pl.BlockSpec(memory_space=pltpu.SMEM)] + [held] * 4,
        out_specs=[held] * len(widths),
        compiler_params=params(16),
        cost_estimate=cost(1.5),
        name="place",
    )(dst.astype(jnp.int32), *pieces)
    return [out.reshape(PLANE * rows, width) for out, width in zip(outs, widths)]


class Gather:
    def __init__(self, shards, dp, core, n_dp):
        self.widths = [shard.shape[1] for shard in shards]
        self.mine = jnp.concatenate(shards, axis=1) if len(shards) > 1 else shards[0]
        self.hops = n_dp == PLANE
        near, far = near_bits(core)
        planes = dp ^ jnp.stack([jnp.zeros_like(near), near, far, near + far])
        self.order = (planes[:, None] ^ jnp.array([[0, 12, 4, 8]], jnp.int32)).reshape(-1)

    def z_far(self, *after):
        if self.hops:
            self.mine = tie(self.mine, *after) if after else self.mine
            self.far = hop(self.mine, 12, 12)

    def z_near(self, *after):
        self.two = self.first = self.second = self.mine
        if self.hops:
            far = tie(self.far, *after) if after else self.far
            self.two = jnp.stack([self.mine, far])
            self.got = hop(self.two, 4, 4)

    def landed(self, *after):
        if self.hops:
            got = tie(self.got, *after) if after else self.got
            self.first = jnp.concatenate([self.two, got], axis=0)

    def across(self, *after):
        if self.hops:
            first = tie(self.first, *after) if after else self.first
            self.second = hop(first, 1, 2)
            self.third = hop(first, 2, 1)

    def corner(self, *after):
        self.last = self.mine
        if self.hops:
            self.second, self.third = lax.optimization_barrier((self.second, self.third) + after)[:2]
            self.last = hop(self.second, 2, 1)

    def finish(self, *after):
        last = tie(self.last, *after) if after else self.last
        if self.hops:
            owns = place(self.order, [self.first, self.second, self.third, last], self.widths)
        else:
            whole = lax.all_gather(last, "dp", axis=0, tiled=True)
            cuts = [sum(self.widths[: i + 1]) for i in range(len(self.widths) - 1)]
            owns = jnp.split(whole, cuts, axis=1)
        return [(own, swap_core(own)) for own in owns]


def block_sum(counts, refs, extras, z):
    refs, start = list(refs), 0
    for count in counts:
        parts, refs = refs[:count], refs[count:]
        width = parts[0].shape[-1]
        cols = slice(start, start + width)
        value = sum(part[z, 0].astype(F32) for part in parts)
        for extra in extras:
            value = value + extra[0, z, :, cols].astype(F32)
        yield cols, value
        start += width


def add_kernel(counts, index, *refs):
    total = sum(counts)
    totals, extras, out = refs[:total], refs[total:-1], refs[-1]
    for z in range(4):
        for cols, value in block_sum(counts, totals, extras, z):
            out[0, z, :, cols] = value.astype(BF16)


def split_kernel(counts, index, *refs):
    total = sum(counts)
    totals, extras = refs[:total], refs[total:-3]
    send, kept, total_ref = refs[-3:]
    for z in range(4):
        for cols, value in block_sum(counts, totals, extras, z):
            total_ref[z, :, cols] = value
    for step in range(2):
        kept[step] = total_ref[index[1 + step]]
        send[step] = total_ref[index[3 + step]].astype(BF16)


def add_blocks(index, totals, extras, split):
    counts = [len(parts) for parts in totals]
    width = sum(parts[0].shape[3] for parts in totals)
    totals = [part for parts in totals for part in parts]
    rows = totals[0].shape[2]
    steps = 1 if split else index.shape[0]
    in_specs = [
        pl.BlockSpec((4, 1, rows, part.shape[3]), lambda j, idx: (0, idx[j], 0, 0)) for part in totals
    ]
    for _, at in extras:
        in_specs.append(pl.BlockSpec((1, 4, rows, width), lambda j, idx, at=at: (at, 0, 0, 0)))
    scratch = []
    if split:
        out_shape = [jax.ShapeDtypeStruct((2, rows, width), kind) for kind in (BF16, F32)]
        out_specs = [pl.BlockSpec((2, rows, width), lambda j, idx: (0, 0, 0))] * 2
        scratch = [pltpu.VMEM((4, rows, width), F32)]
    else:
        out_shape = jax.ShapeDtypeStruct((steps, 4, rows, width), BF16)
        out_specs = pl.BlockSpec((1, 4, rows, width), lambda j, idx: (j, 0, 0, 0))
    return pl.pallas_call(
        functools.partial(split_kernel if split else add_kernel, counts),
        out_shape=out_shape,
        grid_spec=pltpu.PrefetchScalarGridSpec(
            num_scalar_prefetch=1,
            grid=(steps,),
            in_specs=in_specs,
            out_specs=out_specs,
            scratch_shapes=scratch,
        ),
        compiler_params=params(18 if split else 14),
        cost_estimate=cost(steps * rows * width / 1e5),
        name="split_blocks" if split else "add_blocks",
    )(index.astype(jnp.int32), *totals, *[extra for extra, _ in extras])


class Scatter:
    def __init__(self, dp, core, n_dp):
        self.hops = n_dp == PLANE
        self.parts, self.totals = [], []
        if self.hops:
            near, far = near_bits(core)
            plane, self.deep = dp % 4, (dp // 4) ^ jnp.array([0, 3, 1, 2], jnp.int32)
            self.first = jnp.stack([plane ^ near, plane ^ near ^ far])
            self.second = jnp.stack([plane ^ far])
            self.third = jnp.stack([plane])

    def add(self, left, own, other):
        sent = mm_tl(left, other).astype(BF16)
        self.parts.append((left, own, swap_core(sent)))
        return sent

    def chip(self, *after):
        for left, own, got in self.parts:
            own = tie(own, *after) if after else own
            self.totals.append([(mm_tl(left, own) + got.astype(F32)).astype(BF16)])
        self.parts = []
        return [parts[0] for parts in self.totals]

    def across(self, *after):
        if not self.hops:
            self.total = jnp.concatenate([sum(parts) for parts in self.totals], axis=1)
            return self.total
        shape = lambda v: v.reshape(4, 4, v.shape[0] // PLANE, v.shape[1])
        if after:
            self.totals[0][0] = tie(self.totals[0][0], *after)
        self.totals = [[shape(part) for part in parts] for parts in self.totals]
        send = add_blocks(self.first, self.totals, [], False)
        self.near = hop(send, 1, 2)
        return send

    def corner(self, *after):
        if not self.hops:
            return self.total
        self.near = tie(self.near, *after)
        send = add_blocks(self.second, self.totals, [(self.near, 1)], False)
        self.far = hop(send, 2, 1)
        return send

    def z_near(self, *after):
        if not self.hops:
            return self.total
        far = tie(self.far, *after)
        index = jnp.concatenate([self.third, self.deep])
        send, self.kept = add_blocks(index, self.totals, [(self.near, 0), (far, 0)], True)
        self.got = hop(send, 4, 4)
        return send

    def z_far(self, *after):
        if not self.hops:
            return self.total
        got = tie(self.got, *after)
        self.sum = self.kept[0] + got[0].astype(F32)
        send = (self.kept[1] + got[1].astype(F32)).astype(BF16)
        self.got = hop(send, 12, 12)
        return send

    def finish(self, *after):
        if not self.hops:
            return lax.psum_scatter(self.total, "dp", scatter_dimension=0, tiled=True).astype(F32)
        got = tie(self.got, *after) if after else self.got
        return self.sum + got.astype(F32)


def lanes_of(head, rows):
    lane = lax.broadcasted_iota(jnp.int32, (rows, PAIR), 1)
    return (lane < DH) if head == 0 else (lane >= DH)


def stacked(values):
    zero = jnp.zeros_like(values)
    rows = values.shape[0]
    return jnp.concatenate([jnp.where(lanes_of(head, rows), values, zero) for head in range(2)], axis=0)


def unstacked(values):
    rows = values.shape[0] // 2
    return jnp.where(lanes_of(0, rows), values[:rows], values[rows:])


def attend(queries, keys, values, bias):
    scores = mm_tr(stacked(queries * BF16(SCALE)), keys) + bias
    weights = jnp.exp(scores - jnp.max(scores, axis=-1, keepdims=True))
    total = jnp.sum(weights, axis=-1, keepdims=True)
    return unstacked(mm(weights.astype(BF16), values) / total).astype(BF16)


def self_forward_kernel(q_ref, k_ref, v_ref, bias_ref, o_ref):
    chunk = 128
    keys, values = k_ref[...], v_ref[...]
    for start in range(0, SLAB, chunk):
        rows = slice(start, start + chunk)
        bias = bias_ref[rows, :]
        o_ref[rows, :] = attend(q_ref[rows, :], keys, values, jnp.concatenate([bias, bias], axis=0))


def self_forward(projected, bias):
    width = projected.shape[1] // 3
    pairs = width // PAIR
    whole = pl.BlockSpec((SLAB, SLAB), lambda j: (0, 0))
    part = lambda which: pl.BlockSpec((SLAB, PAIR), lambda j, w=which: (0, w * pairs + j))
    scores = 2 * pairs * SLAB * SLAB
    return pl.pallas_call(
        self_forward_kernel,
        out_shape=jax.ShapeDtypeStruct((SLAB, width), BF16),
        grid=(pairs,),
        in_specs=[part(0), part(1), part(2), whole],
        out_specs=pl.BlockSpec((SLAB, PAIR), lambda j: (0, j)),
        compiler_params=params(12),
        cost_estimate=cost(1.5 * pairs),
        name="self_forward",
    )(projected, projected, projected, bias)


def pull_back(queries, keys, values, grad, bias):
    queries = stacked(queries * BF16(SCALE))
    grad = stacked(grad)
    scores = mm_tr(keys, queries) + bias
    weights = jnp.exp(scores - jnp.max(scores, axis=0, keepdims=True))
    weights = weights * (1.0 / jnp.sum(weights, axis=0, keepdims=True))
    grad_weights = mm_tr(values, grad)
    inner = jnp.sum(weights * grad_weights, axis=0, keepdims=True)
    grad_scores = (weights * (grad_weights - inner)).astype(BF16)
    return (
        unstacked(mm_tl(grad_scores, keys)) * SCALE,
        mm(grad_scores, queries),
        mm(weights.astype(BF16), grad),
    )


def self_backward_kernel(meta, q_ref, k_ref, v_ref, g_ref, bias_ref, out_ref):
    chunk = 128
    pairs = out_ref.shape[1] // PAIR // 3
    pair = pl.program_id(0)
    keys, values = k_ref[...], v_ref[...]
    key_total = value_total = 0.0
    parts = []
    for start in range(0, SLAB, chunk):
        rows = slice(start, start + chunk)
        bias = bias_ref[:, rows]
        query_grad, key_grad, value_grad = pull_back(
            q_ref[rows, :], keys, values, g_ref[rows, :], jnp.concatenate([bias, bias], axis=1)
        )
        parts.append(query_grad)
        key_total = key_total + key_grad
        value_total = value_total + value_grad
    for which, grads in enumerate((jnp.concatenate(parts, axis=0), key_total, value_total)):
        cols = pl.ds(pl.multiple_of((which * pairs + pair) * PAIR, PAIR), PAIR)
        out_ref[:, cols] = grads.astype(BF16)


def self_backward(meta, projected, grad, bias):
    half = projected.shape[1] // 3
    pairs = half // PAIR
    part = lambda which: pl.BlockSpec((SLAB, PAIR), lambda j, m, w=which: (0, w * pairs + j))
    scores = 2 * pairs * SLAB * SLAB
    return pl.pallas_call(
        self_backward_kernel,
        out_shape=jax.ShapeDtypeStruct((SLAB, 3 * half), BF16),
        grid_spec=pltpu.PrefetchScalarGridSpec(
            num_scalar_prefetch=1,
            grid=(pairs,),
            in_specs=[
                part(0),
                part(1),
                part(2),
                pl.BlockSpec((SLAB, PAIR), lambda j, m: (0, m[BLOCKS] + j)),
                pl.BlockSpec((SLAB, SLAB), lambda j, m: (0, 0)),
            ],
            out_specs=pl.BlockSpec((SLAB, 3 * half), lambda j, m: (0, 0)),
        ),
        compiler_params=params(12),
        cost_estimate=cost(10),
        name="self_backward",
    )(meta, projected, projected, projected, grad, bias)


def cross_forward_kernel(meta, q_ref, k_ref, v_ref, bias_ref, o_ref):
    for block in range(BLOCKS):
        slot = meta[block]
        own = pl.ds(pl.multiple_of(slot * TXT, TXT), TXT)
        rows = slice(block * ROWS, (block + 1) * ROWS)
        o_ref[rows, :] = attend(q_ref[rows, :], k_ref[own, :], v_ref[own, :], bias_ref[slot])


def text_part(which, pairs, pair_at):
    def index(j, m):
        pair = pair_at(j, m)
        other = jnp.where(pair // pairs == m[BLOCKS] // pairs, 1, 0)
        return (0, (2 * other + which) * pairs + lax.rem(pair, pairs))

    return pl.BlockSpec((ITEMS * TXT, PAIR), index)


def cross_forward(meta, queries, text_kv, bias):
    width = queries.shape[1]
    pairs = width // PAIR
    frames = pl.BlockSpec((SLAB, PAIR), lambda j, m: (0, j))
    part = lambda which: text_part(which, pairs // 2, lambda j, m: j)
    scores = 2 * pairs * SLAB * TXT
    return pl.pallas_call(
        cross_forward_kernel,
        out_shape=jax.ShapeDtypeStruct((SLAB, width), BF16),
        grid_spec=pltpu.PrefetchScalarGridSpec(
            num_scalar_prefetch=1,
            grid=(pairs,),
            in_specs=[
                frames,
                part(0),
                part(1),
                pl.BlockSpec((ITEMS, 1, TXT), lambda j, m: (0, 0, 0)),
            ],
            out_specs=frames,
        ),
        compiler_params=params(8),
        cost_estimate=cost(7),
        name="cross_forward",
    )(meta, queries, text_kv, text_kv, bias)


def cross_backward_kernel(meta, q_ref, k_ref, v_ref, g_ref, bias_ref, dq_ref, dkv_ref, dk_acc, dv_acc):
    pairs = dkv_ref.shape[2] // PAIR // 2
    pair = lax.rem(pl.program_id(0), pairs)
    dk_acc[...] = jnp.zeros_like(dk_acc)
    dv_acc[...] = jnp.zeros_like(dv_acc)
    for block in range(BLOCKS):
        own = pl.ds(pl.multiple_of(meta[block] * TXT, TXT), TXT)
        rows = slice(block * ROWS, (block + 1) * ROWS)
        bias = bias_ref[own, :]
        query_grad, key_grad, value_grad = pull_back(
            q_ref[rows, :], k_ref[own, :], v_ref[own, :], g_ref[rows, :], jnp.concatenate([bias, bias], axis=1)
        )
        dq_ref[rows, :] = query_grad.astype(BF16)
        dk_acc[own, :] += key_grad
        dv_acc[own, :] += value_grad
    dkv_ref[0, :, pl.ds(pl.multiple_of(pair * PAIR, PAIR), PAIR)] = dk_acc[...].astype(BF16)
    dkv_ref[0, :, pl.ds(pl.multiple_of((pairs + pair) * PAIR, PAIR), PAIR)] = dv_acc[...].astype(BF16)


def cross_backward(meta, queries, text_kv, grad, bias):
    width = queries.shape[1]
    pairs = width // PAIR // 2
    pair_at = lambda j, m: lax.rem(m[BLOCKS] + j, 2 * pairs)
    frames = pl.BlockSpec((SLAB, PAIR), lambda j, m: (0, pair_at(j, m)))
    part = lambda which: text_part(which, pairs, pair_at)
    scores = 4 * pairs * SLAB * TXT
    return pl.pallas_call(
        cross_backward_kernel,
        out_shape=[
            jax.ShapeDtypeStruct((SLAB, width), BF16),
            jax.ShapeDtypeStruct((2, ITEMS * TXT, width), BF16),
        ],
        grid_spec=pltpu.PrefetchScalarGridSpec(
            num_scalar_prefetch=1,
            grid=(2 * pairs,),
            in_specs=[
                frames,
                part(0),
                part(1),
                frames,
                pl.BlockSpec((ITEMS * TXT, ROWS), lambda j, m: (0, 0)),
            ],
            out_specs=[
                frames,
                pl.BlockSpec((1, ITEMS * TXT, width), lambda j, m: (1 - j // pairs, 0, 0)),
            ],
            scratch_shapes=[pltpu.VMEM((ITEMS * TXT, PAIR), F32)] * 2,
        ),
        compiler_params=params(12),
        cost_estimate=cost(13.6),
        name="cross_backward",
    )(meta, queries, text_kv, text_kv, grad, bias)


def normed(values):
    center = values - jnp.mean(values, axis=-1, keepdims=True)
    spread = lax.rsqrt(jnp.mean(center * center, axis=-1, keepdims=True) + 1e-06)
    return center * spread, spread


def by_block(values):
    return values.reshape(BLOCKS, ROWS, -1)


def flat(values):
    return values.reshape(SLAB, -1)


def block_at(j, m):
    return lax.rem(2 * m[0] + j, BLOCKS)


def block_specs(width):
    rows = pl.BlockSpec((ROWS, width), lambda j, m: (block_at(j, m), 0))
    mod = lambda which: pl.BlockSpec((1, 1, width), lambda j, m, w=which: (block_at(j, m), 0, w))
    sums = lambda count: pl.BlockSpec((1, count, width), lambda j, m: (block_at(j, m), 0, 0))
    split = [
        pl.BlockSpec((ROWS, width), lambda j, m: (jnp.minimum(j, 1), 0)),
        pl.BlockSpec((ROWS, width), lambda j, m: (jnp.maximum(j - 2, 0), 0)),
    ]
    return rows, mod, sums, split


def write_split(values, kept, sent):
    step = pl.program_id(0)

    @pl.when(step < 2)
    def _():
        kept[...] = values

    @pl.when(step >= 2)
    def _():
        sent[...] = values


def top_kernel(meta, dy_ref, x_ref, branch_ref, gate_ref, kept, sent, grad_ref, sum_ref):
    dy, branch, gate = dy_ref[...].astype(F32), branch_ref[...], gate_ref[0]
    write_split(x_ref[...] + gate * branch, kept, sent)
    grad_ref[...] = (dy * gate).astype(BF16)
    sum_ref[0] = jnp.sum(dy * branch, axis=0, keepdims=True)


def top_stage(meta, grad_out, values, branch, mods):
    width = values.shape[1]
    rows, mod, sums, split = block_specs(width)
    half_shape = jax.ShapeDtypeStruct((SLAB // 2, width), F32)
    return pl.pallas_call(
        top_kernel,
        out_shape=[
            half_shape,
            half_shape,
            jax.ShapeDtypeStruct((SLAB, width), BF16),
            jax.ShapeDtypeStruct((BLOCKS, 1, width), F32),
        ],
        grid_spec=pltpu.PrefetchScalarGridSpec(
            num_scalar_prefetch=1,
            grid=(BLOCKS,),
            in_specs=[rows, rows, rows, mod(8)],
            out_specs=split + [rows, sums(1)],
        ),
        compiler_params=params(8),
        cost_estimate=cost(1),
        name="top_stage",
    )(meta, grad_out, values, branch, mods)


def norm_back(grad, values, scale_by):
    norm, spread = normed(values)
    inner = grad * (1.0 + scale_by)
    back = (
        inner
        - jnp.mean(inner, axis=-1, keepdims=True)
        - norm * jnp.mean(inner * norm, axis=-1, keepdims=True)
    ) * spread
    return back, jnp.sum(grad, axis=0, keepdims=True), jnp.sum(grad * norm, axis=0, keepdims=True)


def middle_kernel(meta, d_ref, x_ref, old_ref, branch_ref, scale_ref, gate_ref, total_ref, grad_ref, sum_ref):
    back, shift_sum, scale_sum = norm_back(d_ref[...], x_ref[...], scale_ref[0])
    total = old_ref[...].astype(F32) + back
    total_ref[...] = total
    grad_ref[...] = (total * gate_ref[0]).astype(BF16)
    gate_sum = jnp.sum(total * branch_ref[...], axis=0, keepdims=True)
    sum_ref[0] = jnp.concatenate([shift_sum, scale_sum, gate_sum], axis=0)


def middle_stage(meta, grad, values, old, branch, mods, which):
    width = values.shape[1]
    rows, mod, sums, _ = block_specs(width)
    return pl.pallas_call(
        middle_kernel,
        out_shape=[
            jax.ShapeDtypeStruct((SLAB, width), F32),
            jax.ShapeDtypeStruct((SLAB, width), BF16),
            jax.ShapeDtypeStruct((BLOCKS, 3, width), F32),
        ],
        grid_spec=pltpu.PrefetchScalarGridSpec(
            num_scalar_prefetch=1,
            grid=(BLOCKS,),
            in_specs=[rows, rows, rows, rows, mod(3 * which + 1), mod(3 * which - 1)],
            out_specs=[rows, rows, sums(3)],
        ),
        compiler_params=params(10),
        cost_estimate=cost(2),
        name="middle_stage",
    )(meta, grad, values, old, branch, mods, mods)


def bottom_kernel(meta, d_ref, x_ref, old_ref, scale_ref, kept, sent, sum_ref):
    back, shift_sum, scale_sum = norm_back(d_ref[...], x_ref[...].astype(F32), scale_ref[0])
    write_split(old_ref[...] + back, kept, sent)
    sum_ref[0] = jnp.concatenate([shift_sum, scale_sum], axis=0)


def bottom_stage(meta, grad, values, old, mods):
    width = values.shape[1]
    rows, mod, sums, split = block_specs(width)
    half_shape = jax.ShapeDtypeStruct((SLAB // 2, width), F32)
    return pl.pallas_call(
        bottom_kernel,
        out_shape=[half_shape, half_shape, jax.ShapeDtypeStruct((BLOCKS, 2, width), F32)],
        grid_spec=pltpu.PrefetchScalarGridSpec(
            num_scalar_prefetch=1,
            grid=(BLOCKS,),
            in_specs=[rows, rows, rows, mod(1)],
            out_specs=split + [sums(2)],
        ),
        compiler_params=params(8),
        cost_estimate=cost(2),
        name="bottom_stage",
    )(meta, grad, values, old, mods)


ROOT = math.sqrt(2.0 / math.pi)


def gelu_parts(values):
    square = values * values
    bent = jnp.tanh(ROOT * values * (1.0 + 0.044715 * square))
    slope = 0.5 * (1.0 + bent) + 0.5 * values * (1.0 - bent * bent) * (
        ROOT * (1.0 + 3.0 * 0.044715 * square)
    )
    return 0.5 * values * (1.0 + bent), slope


def time_embed(timesteps, width):
    halfwidth = width // 2
    frequency = jnp.exp(-math.log(10000.0) * jnp.arange(halfwidth).astype(F32) / halfwidth)
    angles = timesteps.astype(F32)[:, None] * frequency[None, :]
    return jax.nn.silu(jnp.concatenate([jnp.cos(angles), jnp.sin(angles)], axis=-1))


def time_features(timesteps, feature, width):
    halfwidth = width // 2
    place = jnp.where(feature < halfwidth, feature, feature - halfwidth)
    frequency = jnp.exp(-math.log(10000.0) * place.astype(F32) / halfwidth)
    angles = timesteps.astype(F32)[:, None] * frequency
    return jax.nn.silu(jnp.where(feature < halfwidth, jnp.cos(angles), jnp.sin(angles)))


def per_device(
    frames,
    text_states,
    cotangent,
    item_lengths,
    text_lengths,
    timesteps,
    w_qkv,
    w_proj,
    w_query,
    w_cproj,
    w_ada,
    b_ada,
    w_kv,
    w_up,
    w_down,
):
    n_dp = lax.axis_size("dp")
    n_all = n_dp * lax.axis_size("head")
    dp, core = lax.axis_index("dp"), lax.axis_index("head")
    width = frames.shape[2]
    half = width // 2
    thin = w_qkv.shape[0]

    def pick(pair):
        return jnp.where(core == 0, pair[0], pair[1])

    def join(own, other, axis):
        return jnp.where(
            core == 0,
            jnp.concatenate([own, other], axis=axis),
            jnp.concatenate([other, own], axis=axis),
        )

    def part(values, size, which, axis):
        return lax.dynamic_slice_in_dim(values, which * size, size, axis)

    def own_frames(values):
        kept, sent = pick((values[0], values[1])), pick((values[1], values[0]))
        return join(kept, swap_core(sent), 0)

    def halves(values, axis):
        low, high = jnp.split(values, 2, axis=axis)
        return pick((low, high)), swap_core(pick((high, low)))

    def both(kept, got):
        return join(kept[None], got[None], 0)

    gather = lambda *shards: Gather(shards, dp, core, n_dp)
    kept_half, sent = cut(core, [w_qkv, w_proj, w_query, w_cproj], [3, 1, 1, 1])
    got = swap_core(sent)

    lane_tiles = w_ada.shape[1] // 128
    ada_cols = 128 * (-(-lane_tiles // n_all))
    owners = w_ada.shape[1] // ada_cols
    bias_cols = b_ada.shape[0]
    steps_here = timesteps.reshape(1, -1)
    coded = jnp.concatenate([steps_here // 32, steps_here % 32], axis=1).astype(BF16)
    coded = jnp.concatenate(
        [
            jnp.pad(coded, ((0, 0), (0, ada_cols - coded.shape[1]))),
            jnp.pad(b_ada[None], ((0, 0), (0, ada_cols - bias_cols))),
        ],
        axis=0,
    )
    packed = tie(w_ada, sent).reshape(thin, owners, ada_cols).transpose(1, 0, 2)
    packed = jnp.concatenate(
        [
            jnp.pad(packed, ((0, n_all - owners), (0, 0), (0, 0))),
            jnp.broadcast_to(coded[None], (n_all,) + coded.shape),
        ],
        axis=1,
    )
    shared = join(kept_half, tie(got, packed), 0)
    qkv_shard, proj_shard, query_shard, cproj_shard = jnp.split(
        shared, [3 * half, 4 * half, 5 * half], axis=1
    )
    gather_self = gather(qkv_shard, proj_shard)
    gather_self.z_far()
    got_cols = lax.all_to_all(
        tie(packed, gather_self.mine), BOTH, split_axis=0, concat_axis=0, tiled=True
    )
    kv_shard = jnp.concatenate([tie(w_kv[0], gather_self.mine), w_kv[1]], axis=1)
    gather_one = gather(kv_shard, query_shard, cproj_shard)
    gather_one.z_far()
    frames_here = own_frames(tie(frames, gather_one.mine))
    gather_self.z_near(frames_here)
    gather_one.z_near(gather_self.two)
    gather_up = gather(tie(w_up, gather_one.two))
    gather_up.z_far()
    gather_self.landed(gather_up.mine)
    gather_self.across()
    got_cols = tie(got_cols, gather_self.first)
    ada_part = got_cols[:, :thin].reshape(width, ada_cols)
    digits = got_cols[:, thin, : 4 * ITEMS].astype(F32).reshape(n_dp, 2, 2, 2 * ITEMS)[:, 0]
    all_steps = (digits[:, 0] * 32.0 + digits[:, 1]).reshape(n_all * ITEMS)
    embedding = time_embed(all_steps, width)
    all_mods = jnp.dot(embedding, ada_part.astype(F32), precision=PRECISE)
    all_mods = all_mods.reshape(n_all, ITEMS, ada_cols)
    got_mods = lax.all_to_all(all_mods, BOTH, split_axis=0, concat_axis=0, tiled=True)
    ada_bias = got_cols[:, thin + 1, :bias_cols].reshape(9 * width).astype(F32)

    gather_one.landed(all_mods)
    gather_up.z_near(gather_one.first)
    gather_down = gather(tie(w_down, gather_up.two).T)
    gather_down.z_far()
    gather_self.corner(gather_up.two)
    gather_one.across(gather_self.second)
    item_mods = got_mods[:owners].transpose(1, 0, 2).reshape(ITEMS, 9 * width) + ada_bias

    text_rows = lax.dynamic_index_in_dim(text_states, core, 0, keepdims=False).reshape(ITEMS * TXT, width)
    residual = by_block(frames_here.astype(F32))
    grad_out = own_frames(tie(cotangent, all_mods))
    item_lengths, text_lengths = lax.optimization_barrier((item_lengths, text_lengths, all_mods))[:2]
    lengths = lax.dynamic_index_in_dim(item_lengths, core, 0, keepdims=False)[0]
    text_counts = lax.dynamic_index_in_dim(text_lengths, core, 0, keepdims=False)[0]

    item_count = jnp.sum((lengths > 0).astype(jnp.int32))
    nominal = SLAB // item_count
    slots = jnp.arange(ITEMS, dtype=jnp.int32)
    block_slot = (jnp.arange(BLOCKS, dtype=jnp.int32) * ROWS) // nominal
    block_hot = block_slot[:, None] == slots[None, :]
    position = jnp.arange(SLAB, dtype=jnp.int32)
    frame_slot = position // nominal
    own_length = jnp.sum(
        jnp.where(frame_slot[:, None] == slots[None, :], lengths[None, :], 0), axis=1
    )
    frame_live = position - frame_slot * nominal < own_length
    same = frame_slot[:, None] == frame_slot[None, :]
    self_bias = jnp.where(same & frame_live[None, :], 0.0, MASKED).astype(F32)
    self_bias_back = jnp.where(same & frame_live[:, None], 0.0, MASKED).astype(F32)
    text_live = jnp.arange(TXT, dtype=jnp.int32)[None, :] < text_counts[:, None]
    cross_bias = jnp.where(text_live, 0.0, MASKED).astype(F32)
    cross_bias_back = jnp.broadcast_to(cross_bias.reshape(ITEMS * TXT, 1), (ITEMS * TXT, ROWS))
    cross_bias = cross_bias[:, None, :]
    pairs = half // PAIR
    metas = [
        jnp.concatenate([block_slot, jnp.full((1,), pairs, jnp.int32) * side]).astype(jnp.int32)
        for side in (core, 1 - core)
    ]

    mods = jnp.sum(jnp.where(block_hot[:, :, None], item_mods[None], 0.0), axis=1)
    (
        shift_one,
        scale_one,
        gate_one,
        shift_two,
        scale_two,
        gate_two,
        shift_three,
        scale_three,
        gate_three,
    ) = [piece[:, None, :] for piece in jnp.split(mods, 9, axis=1)]

    def features_of(steps, side):
        column = lax.broadcasted_iota(jnp.int32, (1, thin + 1), 1)
        feature = (2 * dp + side) * thin + column
        return jnp.where(column < thin, time_features(steps, feature, width), 1.0)

    by_core = all_steps.reshape(n_dp, 2, ITEMS)
    slot_steps = pick((by_core[:, 0], by_core[:, 1])).reshape(n_dp * ITEMS)
    own_features, other_features = [features_of(slot_steps, side) for side in (core, 1 - core)]
    all_features = features_of(all_steps, core)

    norm_one, _ = normed(residual)
    hidden_one = flat(norm_one * (1.0 + scale_one) + shift_one).astype(BF16)
    w_qkvs, w_projs = gather_self.finish(hidden_one, gather_one.second)
    gather_one.corner(w_qkvs[0])
    gather_up.landed(gather_one.second)
    gather_up.across()
    projected = [mm(tie(hidden_one, gather_up.first), w_qkvs[0]).astype(BF16)]
    gather_down.z_near(projected[0])
    outs = [self_forward(tie(projected[0], gather_down.two), self_bias)]
    gather_down.landed(outs[0])
    projected.append(mm(tie(hidden_one, outs[0]), w_qkvs[1]).astype(BF16))
    outs.append(self_forward(projected[1], self_bias))
    w_kvs, w_queries, w_cprojs = gather_one.finish(outs[1])
    gather_up.corner(outs[1])
    gather_down.across(gather_up.second)
    attended = join(outs[0], tie(outs[1], w_kvs[0], gather_up.second), 1)
    proj_full = join(*w_projs, 1)
    branch_one = by_block(mm(attended, proj_full))
    after_one = residual + gate_one * branch_one
    norm_two, _ = normed(after_one)
    hidden_two = flat(norm_two * (1.0 + scale_two) + shift_two).astype(BF16)
    query_full, cproj_full = [join(*pair, 1) for pair in (w_queries, w_cprojs)]
    text_kv = mm(tie(text_rows, hidden_two), jnp.concatenate(w_kvs, axis=1)).astype(BF16)
    queries = mm(hidden_two, query_full).astype(BF16)
    crossed = cross_forward(metas[1], queries, text_kv, cross_bias)
    (w_ups,) = gather_up.finish(crossed)
    gather_down.corner(crossed)
    branch_two = by_block(mm(crossed, cproj_full))
    after_two = after_one + gate_two * branch_two
    norm_three, _ = normed(after_two)
    hidden_three = flat(norm_three * (1.0 + scale_three) + shift_three).astype(BF16)
    hidden_three = tie(hidden_three, gather_down.second)
    active, slopes = zip(*[gelu_parts(mm(hidden_three, weight)) for weight in w_ups])
    active, slopes = [[value.astype(BF16) for value in values] for values in (active, slopes)]
    (w_downs,) = gather_down.finish(active[0])
    branch_three = mm_tr(active[0], w_downs[0]) + mm_tr(active[1], w_downs[1])
    mods = mods[:, None, :]
    here = jnp.stack([core]).astype(jnp.int32)
    kept_out, sent_out, grad_down, sums_top = top_stage(here, grad_out, flat(after_two), branch_three, mods)
    got_out = swap_core(sent_out)

    def columns(values):
        return [part(values, half, core, 1), part(values, half, 1 - core, 1)]

    def by_item(*grads):
        grads = jnp.concatenate(grads, axis=1).reshape(BLOCKS, -1)
        return jnp.sum(jnp.where(block_hot[:, :, None], grads[:, None, :], 0.0), axis=0).astype(BF16)

    def to_all(items, axes, count):
        copies = jnp.broadcast_to(items[None], (count,) + items.shape)
        return copies, lax.all_to_all(copies, axes, split_axis=0, concat_axis=0, tiled=True)

    def ada_rows(features, items):
        items = items.reshape(features.shape[0], -1).astype(F32)
        return lax.dot_general(
            features, items, (((0,), (0,)), ((), ())), precision=PRECISE, preferred_element_type=F32
        )

    sum_ff, sum_cross, sum_self = [Scatter(dp, core, n_dp) for _ in range(3)]

    sent = sum_ff.add(grad_down, active[0], active[1])
    grad_ups = [
        (mm(tie(grad_down, sent), weight) * slope.astype(F32)).astype(BF16)
        for weight, slope in zip(w_downs, slopes)
    ]
    sent = sum_ff.add(hidden_three, grad_ups[0], grad_ups[1])
    grad_ups = [tie(grad, sent) for grad in grad_ups]
    grad_hidden = mm_tr(grad_ups[0], w_ups[0]) + mm_tr(grad_ups[1], w_ups[1])

    grad_two, grad_cproj, sums_three = middle_stage(
        here, grad_hidden, flat(after_two), grad_out, flat(branch_two), mods, 2
    )
    sums = sum_ff.chip(grad_cproj)
    grad_crossed = mm_tr(tie(grad_cproj, *sums), cproj_full).astype(BF16)
    block_out = both(kept_out, got_out)
    sent = sum_ff.across(grad_crossed, block_out)
    grad_crossed = tie(grad_crossed, sent)
    grad_query, grad_kvs = cross_backward(metas[1], queries, text_kv, grad_crossed, cross_bias_back)
    sum_cross.add(crossed, *columns(grad_cproj))
    sum_cross.add(hidden_two, *columns(grad_query))
    sent = sum_cross.add(text_rows, grad_kvs[0], grad_kvs[1])
    grad_hidden = mm_tr(tie(grad_query, sent), query_full)

    grad_one, grad_proj, sums_two = middle_stage(
        here, grad_hidden, flat(after_one), grad_two, flat(branch_one), mods, 1
    )
    sums = sum_cross.chip(grad_proj)
    sent = sum_ff.corner(*sums)
    grad_proj = tie(grad_proj, sent)
    sent = sum_cross.add(attended, *columns(grad_proj))
    grad_attended = mm_tr(tie(grad_proj, sent), proj_full).astype(BF16)
    grad_kvs = tie(grad_kvs, grad_attended)
    grad_text = (mm_tr(grad_kvs[0], w_kvs[0]) + mm_tr(grad_kvs[1], w_kvs[1])).astype(BF16)
    text_halves = halves(grad_text.reshape(ITEMS, TXT, width), 1)
    early_items = by_item(
        sums_two[:, 2:], sums_two[:, :2], sums_three[:, 2:], sums_three[:, :2], sums_top
    )
    early_copies, early_items = to_all(early_items, "dp", n_dp)
    sum_cross.chip(text_halves[0])
    sent = sum_cross.across(grad_attended, early_copies)
    sent = sum_ff.z_near(sent)
    other = self_backward(metas[1], projected[1], tie(grad_attended, sent), self_bias_back)
    sent = sum_cross.corner(other)
    other = tie(other, sent)
    crossing = mm_tl(hidden_one, other).astype(BF16)
    sent = sum_ff.z_far(crossing)
    own = self_backward(metas[0], projected[0], tie(grad_attended, sent), self_bias_back)
    sum_self.totals.append([mm_tl(hidden_one, own).astype(BF16), swap_core(crossing)])
    sent = sum_self.across()
    own, other = lax.optimization_barrier((own, other, sent))[:2]
    grad_hidden = mm_tr(own, w_qkvs[0]) + mm_tr(other, w_qkvs[1])
    sent = sum_cross.z_near(grad_hidden)
    text_grad = both(tie(text_halves[0], grad_hidden), text_halves[1]).astype(F32)
    sent = sum_self.corner(grad_hidden, sent, text_grad)
    grad_hidden = tie(grad_hidden, sent)
    kept_in, sent_in, sums_one = bottom_stage(here, grad_hidden, frames_here, grad_one, mods)
    got_in = swap_core(sent_in)

    late_copies, late_items = to_all(by_item(sums_one), BOTH, n_all)
    sent = sum_self.z_near(late_copies)
    sent = sum_cross.z_far(sent)
    early_items = tie(early_items, sent)
    early_rows = ada_rows(own_features, early_items)
    early_sent = ada_rows(other_features, early_items)
    sent = sum_self.z_far(early_sent)
    frames_grad = both(tie(kept_in, sent), got_in)
    late_rows = ada_rows(all_features, tie(late_items, sent))
    ada_sum = jnp.concatenate([late_rows, early_rows + swap_core(early_sent)], axis=1)
    bias_sum = lax.dynamic_slice_in_dim(ada_sum[thin], (2 * dp + core) * bias_cols, bias_cols, 0)
    ada_sum = ada_sum[:thin]

    def own_rows(values):
        kept = part(values, thin, core, 0)
        got = swap_core(part(values, thin, 1 - core, 0))
        return join(kept, got, 1)

    ff_sum = sum_ff.finish(own)
    down_sum, up_sum = jnp.split(ff_sum, [2 * width], axis=1)
    cross_sum = sum_cross.finish(sent)
    cproj_part, query_part, kv_part, proj_part = jnp.split(
        cross_sum, [half, 2 * half, 4 * half], axis=1
    )
    kv_grad = jnp.stack(jnp.split(kv_part, 2, axis=1))
    qkv_grad = own_rows(sum_self.finish(frames_grad, ada_sum, bias_sum))
    qkv_grad = qkv_grad.reshape(thin, 2, 3, half).transpose(0, 2, 1, 3).reshape(thin, 3 * width)
    return (
        block_out,
        frames_grad,
        text_grad[:, None],
        qkv_grad,
        own_rows(proj_part),
        own_rows(query_part),
        own_rows(cproj_part),
        ada_sum,
        bias_sum,
        kv_grad,
        up_sum,
        down_sum.T,
    )


def solution(mesh):
    return jax.shard_map(
        per_device,
        mesh=mesh,
        in_specs=(
            P(None, ("dp", "head"), None),
            P(None, "dp", None, None, None),
            P(None, ("dp", "head"), None),
            P(None, "dp", None),
            P(None, "dp", None),
            P(None, "dp", None),
            P(("dp", "head"), None),
            P(("dp", "head"), None),
            P(("dp", "head"), None),
            P(("dp", "head"), None),
            P(("dp", "head"), None),
            P(("dp", "head")),
            P(None, "dp", "head"),
            P("dp", "head"),
            P("head", "dp"),
        ),
        out_specs=(
            P(None, ("dp", "head"), None),
            P(None, ("dp", "head"), None),
            P(None, "dp", None, "head", None),
            P(("dp", "head"), None),
            P(("dp", "head"), None),
            P(("dp", "head"), None),
            P(("dp", "head"), None),
            P(("dp", "head"), None),
            P(("dp", "head")),
            P(None, "dp", "head"),
            P("dp", "head"),
            P("head", "dp"),
        ),
        check_vma=False,
    )
```

time: 1810 us -> 358 us (0.20)
  waiting for transfers between devices: 1040 us -> 39.1 us
  matrix products: 272 us -> 76.8 us
  blocking collectives: 168 us -> 0 us
  local copies, waits for them, and re-layouts: 162 us -> 37.9 us
  other arithmetic: 129 us -> 39.4 us
  Pallas kernels: 0 us -> 78.4 us
  starting transfers between devices: 2.35 us -> 76.5 us
    reduce_scatter x13 -> x0, waiting for transfers between devices: 821 us -> none  [the longest x1 227 us: per_device(): lax.psum_scatter(shared_grads[4], ('dp', 'head'), scatter_dimension=0, ti...]
    all_gather x8 -> x0, waiting for transfers between devices: 217 us -> none  [the longest x1 83.1 us: per_device(): lax.all_gather(w_ada, ('dp', 'head'), axis=0, tiled=True)]
    dot_general x74 -> x39, matrix products: 272 us -> 76.8 us  [the longest x10 27.5 us: mm(): return jnp.dot(left, right, preferred_element_type=F32)]
    unnamed x2 -> x0, blocking collectives: 83.4 us -> none
    pallas_call x0 -> x24, Pallas kernels: none -> 78.4 us  [the longest x2 20 us: self_backward(): pl.pallas_call(self_backward_kernel, out_shape=jax.ShapeDtypeStruct((SLAB...]
    all_to_all x16 -> x0, blocking collectives: 74.6 us -> none  [the longest x8 38.7 us: to_heads(): lax.all_to_all(values, 'head', split_axis=2, concat_axis=1, tiled=True)]
    ppermute x0 -> x57, starting transfers between devices: none -> 57.1 us  [the longest x32 52 us: hop(): return lax.ppermute(values, BOTH, pairs)]
    unnamed x401 -> x216, local copies, waits for them, and re-layouts: 65.4 us -> 13.4 us
  transfers between devices with their start and end apart: 22 -> 61, of which waited for: 13 -> 11; matrix products, arithmetic and copies ran while one was open for 23% -> 37% of each run, Pallas kernels for 0% -> 21%
where the time goes in v1:
time: 358 us; the launch traced here: 353 us
  Pallas kernels  78.4 us (22%)
  matrix products  76.8 us (21%)
  starting transfers between devices  76.5 us (21%)
  other arithmetic  39.4 us (11%)
  waiting for transfers between devices  39.1 us (11%)
  local copies, waits for them, and re-layouts  37.9 us (11%)
  between operations  4.8 us (1%)
    ppermute x32, starting transfers between devices, hop(): return lax.ppermute(values, BOTH, pairs)  52 us
    ppermute x32, waiting for transfers between devices, hop(): return lax.ppermute(values, BOTH, pairs)  36.3 us
    dot_general x10, matrix products, mm(): return jnp.dot(left, right, preferred_element_type=F32)  27.5 us
    dot_general x11, matrix products, mm_tr(): lax.dot_general(left, right, (((1,), (1,)), ((), ())), preferred_element_...  21.9 us
    dot_general x14, matrix products, mm_tl(): lax.dot_general(left, right, (((0,), (0,)), ((), ())), preferred_element_...  20.2 us
    pallas_call x2, Pallas kernels, self_backward(): pl.pallas_call(self_backward_kernel, out_shape=jax.ShapeDtypeStruct((SLAB...  20 us
    pallas_call x9, Pallas kernels, add_blocks(): pl.pallas_call(functools.partial(split_kernel if split else add_kernel, c...  16 us
    pallas_call x1, Pallas kernels, cross_backward(): pl.pallas_call(cross_backward_kernel, out_shape=[jax.ShapeDtypeStruct((SL...  14 us
  transfers between devices with their start and end apart: 61, of which 11 were waited for; matrix products, arithmetic and copies ran while one was open for 37% of the time, Pallas kernels for 21%

profile of v1, /device:TPU:0, one launch (start us, length us, event | category | flops | bytes accessed | tf_op | source)
XLA Modules:
  0.0 352.8 jit_solution(1895274143134158384)
XLA Ops:
  11.4 5.0 %collective-permute-start.1 = (bf16[48,1536]{1,0:T(8,128)(2,1)S(1)}, bf16[48,1536]{1,0:T(8,128)(2,1)S(1)}, u32[]{:S(2)}, u32[]{:S(2)}) collective-permute-start(bf16[48,1536]{1,0:T(8,128)(2,1)S(1)} %get-tuple-element.250), channel_id=1, source_target_pairs={{0,24},{1,25},{2,26},{3,27},{4,28},{5,29},{6,30},{7,31},{8,16},{9,... | collective-permute-start | bytes 442376 | tf_op jit(solution)/shard_map/ppermute | solution.py:58
  17.6 6.1 %all-to-all-start = ((bf16[32,26,256]{2,1,0:T(8,128)(2,1)}), bf16[32,26,256]{2,1,0:T(8,128)(2,1)S(1)}, u32[]{:S(2)}, u32[]{:S(2)}) async-start(bf16[32,26,256]{2,1,0:T(8,128)(2,1)} %copy.55), calls=%async_computation | async-start | bytes 1048576 | tf_op jit(solution)/shard_map/all_to_all | solution.py:761
  28.5 7.4 %collective-permute-start.7 = (bf16[2,48,1536]{2,1,0:T(8,128)(2,1)}, bf16[2,48,1536]{2,1,0:T(8,128)(2,1)}, u32[]{:S(2)}, u32[]{:S(2)}) collective-permute-start(bf16[2,48,1536]{2,1,0:T(8,128)(2,1)} %pad_maximum_fusion.7), channel_id=1, source_target_pairs={{0,8},{1,9},{2,10},{3,11},{4,12},{5,13},{6,14},{7,15},{8,0},{9,1},... | collective-permute-start | bytes 884744 | tf_op jit(solution)/shard_map/ppermute | solution.py:58
  36.0 3.5 collective-permute-start.6
  53.3 3.6 %all-to-all-start.1 = ((f32[32,4,256]{2,1,0:T(4,128)}), f32[32,4,256]{2,1,0:T(4,128)}, u32[]{:S(2)}, u32[]{:S(2)}) async-start(f32[32,4,256]{2,1,0:T(4,128)} %copy.57), calls=%async_computation.1 | async-start | bytes 262144 | tf_op jit(solution)/shard_map/all_to_all | solution.py:781
  60.7 2.4 collective-permute-start.14
  69.4 12.2 %collective-permute-done.13.refs_3_ = bf16[4,48,1536]{2,1,0:T(8,128)(2,1)S(1)} collective-permute-done((bf16[4,48,1536]{2,1,0:T(8,128)(2,1)S(1)}, bf16[4,48,1536]{2,1,0:T(8,128)(2,1)S(1)}, u32[]{:S(2)}, u32[]{:S(2)}) %collective-permute-start.13) | collective-permute-done | bytes 589856 | tf_op jit(solution)/shard_map/ppermute | solution.py:58
  86.0 1.9 collective-permute-done.12.refs_2_
  93.7 4.4 %self_forward.2 = bf16[512,384]{1,0:T(8,128)(2,1)S(1)} custom-call(bf16[512,1152]{1,0:T(8,128)(2,1)S(1)} %convolution_convert_fusion.6.q_ref.k_ref.v_ref, bf16[512,1152]{1,0:T(8,128)(2,1)S(1)} %convolution_convert_fusion.6.q_ref.k_ref.v_ref, bf16[512,1152]{1,0:T(8,128)(2,1)S(1)} %convolution_convert_fusion.6.q_ref.k_ref.v_ref, ...), custom_call_target="tpu_custom_call" | custom-call | flops 4950000128 | bytes 15750000 | tf_op jit(solution)/shard_map/self_forward/pallas_call | solution.py:344
  98.1 2.7 collective-permute-done.23
  102.1 4.4 %self_forward.3 = bf16[512,384]{1,0:T(8,128)(2,1)S(1)} custom-call(bf16[512,1152]{1,0:T(8,128)(2,1)S(1)} %convolution_convert_fusion.5.q_ref.k_ref.v_ref, bf16[512,1152]{1,0:T(8,128)(2,1)S(1)} %convolution_convert_fusion.5.q_ref.k_ref.v_ref, bf16[512,1152]{1,0:T(8,128)(2,1)S(1)} %convolution_convert_fusion.5.q_ref.k_ref.v_ref, ...), custom_call_target="tpu_custom_call" | custom-call | flops 4950000128 | bytes 15750000 | tf_op jit(solution)/shard_map/self_forward/pallas_call | solution.py:344
  108.0 2.5 collective-permute-done.18.refs_2_
  113.7 2.1 fusion.126
  118.3 2.9 convolution_convert_fusion.k_ref.v_ref
  121.3 7.4 %cross_forward.1 = bf16[512,768]{1,0:T(8,128)(2,1)S(1)} custom-call(s32[5]{0:T(128)S(1)} %get-tuple-element.274.meta, bf16[512,768]{1,0:T(8,128)(2,1)S(1)} %convolution_convert_fusion.9.q_ref, bf16[1024,1536]{1,0:T(8,128)(2,1)S(1)} %convolution_convert_fusion.k_ref.v_ref, bf16[1024,1536]{1,0:T(8,128)(2,1)S(1)} %convolution_convert_fusion.k_ref.v_ref, ...), custom_call_target="tpu_custom_call" | custom-call | flops 7699999744 | bytes 24500000 | tf_op jit(solution)/shard_map/cross_forward/pallas_call | solution.py:442
  129.7 2.0 fusion.124
  132.3 2.1 place.6
  134.7 5.7 %multiply_convert_fusion.1 = (bf16[512,1536]{1,0:T(8,128)(2,1)}, f32[512,1536]{1,0:T(8,128)}) fusion(bf16[512,768]{1,0:T(8,128)(2,1)S(1)} %fusion.17, bf16[768,1536]{1,0:T(8,128)(2,1)} %bitcast.46), kind=kOutput, calls=%fused_computation.15 | convolution fusion | flops 1215037440 | bytes 7864320 | tf_op jit(solution)/shard_map/dot_general | solution.py:40
  140.3 2.1 place.7
  149.3 3.2 fusion.129
  152.5 3.0 fusion.130
  155.5 3.7 %convolution_add_fusion.3.branch_ref = f32[512,768]{1,0:T(8,128)S(1)} fusion(f32[512,768]{1,0:T(8,128)S(1)} %fusion.129, bf16[768,1536]{1,0:T(8,128)(2,1)} %collective-permute-done.29, f32[512,1536]{1,0:T(8,128)S(1)} %fusion.130), kind=kOutput, calls=%fused_computation.61 | convolution fusion | flops 1215430656 | bytes 8650752 | tf_op jit(solution)/shard_map/dot_general | solution.py:48
  162.0 4.3 %fusion.1 = bf16[512,1536]{1,0:T(8,128)(2,1)S(1)} fusion(bf16[512,768]{1,0:T(8,128)(2,1)S(1)} %get-tuple-element.167, bf16[768,1536]{1,0:T(8,128)(2,1)} %collective-permute-done.29, f32[512,1536]{1,0:T(8,128)S(1)} %fusion.130), kind=kOutput, calls=%fused_computation.20 | convolution fusion | flops 1223688192 | bytes 7864320 | tf_op jit(solution)/shard_map/dot_general | solution.py:40
  168.3 4.2 %fusion = bf16[512,1536]{1,0:T(8,128)(2,1)S(1)} fusion(bf16[512,768]{1,0:T(8,128)(2,1)S(1)} %get-tuple-element.167, bf16[768,1536]{1,0:T(8,128)(2,1)} %bitcast.47, f32[512,1536]{1,0:T(8,128)S(1)} %copy-done.105), kind=kOutput, calls=%fused_computation.19 | convolution fusion | flops 1223688192 | bytes 7864320 | tf_op jit(solution)/shard_map/dot_general | solution.py:40
  172.5 3.1 fusion.131
  175.6 3.2 convolution_add_fusion.2.d_ref
  189.4 2.2 add_blocks.6
  193.0 14.0 %cross_backward.1 = (bf16[512,768]{1,0:T(8,128)(2,1)S(1)}, bf16[2,1024,768]{2,1,0:T(8,128)(2,1)S(1)}) custom-call(s32[5]{0:T(128)S(1)} %get-tuple-element.274.meta, bf16[512,768]{1,0:T(8,128)(2,1)S(1)} %copy-done.52, bf16[1024,1536]{1,0:T(8,128)(2,1)S(1)} %copy-done.55, bf16[1024,1536]{1,0:T(8,128)(2,1)S(1)} %copy-done.55, ...), custom_call_target="tpu_custom_call" | custom-call | flops 14960000000 | bytes 47600000 | tf_op jit(solution)/shard_map/cross_backward/pallas_call | solution.py:488
  207.0 2.5 fusion.23
  222.8 2.9 add_convert_fusion.5
  225.7 3.1 add_blocks.7
  238.9 1.9 add_blocks.8
  248.6 4.7 %all-to-all-start.2 = ((bf16[16,4,5376]{2,1,0:T(4,128)(2,1)}), bf16[16,4,5376]{2,1,0:T(4,128)(2,1)}, u32[]{:S(2)}, u32[]{:S(2)}) async-start(bf16[16,4,5376]{2,1,0:T(4,128)(2,1)} %broadcast_in_dim.244), calls=%async_computation.2 | async-start | bytes 1376256 | tf_op jit(solution)/shard_map/all_to_all | solution.py:896
  255.0 3.1 split_blocks.3
  258.1 2.0 collective-permute-start.39
  260.1 10.0 %self_backward.2 = bf16[512,1152]{1,0:T(8,128)(2,1)S(1)} custom-call(s32[5]{0:T(128)S(1)} %get-tuple-element.274.meta, bf16[512,1152]{1,0:T(8,128)(2,1)S(1)} %copy-done.50, bf16[512,1152]{1,0:T(8,128)(2,1)S(1)} %copy-done.50, bf16[512,1152]{1,0:T(8,128)(2,1)S(1)} %copy-done.50, bf16[512,768]{1,0:T(8,128)(2,1)S(1)} %copy-done.53, f32[512,512]{1,0:T(8,128)S(1)} %copy-done.18), custom_call_target="tpu_custom_call" | custom-call | flops 11000000512 | bytes 35000000 | tf_op jit(solution)/shard_map/self_backward/pallas_call | solution.py:398
  274.4 4.7 %collective-permute-done.39 = bf16[2,48,3072]{2,1,0:T(8,128)(2,1)S(1)} collective-permute-done((bf16[2,48,3072]{2,1,0:T(8,128)(2,1)S(1)}, bf16[2,48,3072]{2,1,0:T(8,128)(2,1)S(1)}, u32[]{:S(2)}, u32[]{:S(2)}) %collective-permute-start.39) | collective-permute-done | bytes 589856 | tf_op jit(solution)/shard_map/ppermute | solution.py:58
  279.2 3.1 collective-permute-start.56
  282.3 10.0 %self_backward.3 = bf16[512,1152]{1,0:T(8,128)(2,1)S(1)} custom-call(s32[5]{0:T(128)S(1)} %get-tuple-element.273.meta, bf16[512,1152]{1,0:T(8,128)(2,1)S(1)} %copy-done.48, bf16[512,1152]{1,0:T(8,128)(2,1)S(1)} %copy-done.48, bf16[512,1152]{1,0:T(8,128)(2,1)S(1)} %copy-done.48, bf16[512,768]{1,0:T(8,128)(2,1)S(1)} %copy-done.53, f32[512,512]{1,0:T(8,128)S(1)} %copy-done.18), custom_call_target="tpu_custom_call" | custom-call | flops 11000000512 | bytes 35000000 | tf_op jit(solution)/shard_map/self_backward/pallas_call | solution.py:398
  298.8 2.0 split_blocks.4
  301.8 6.0 %collective-permute-done.42.refs_2_ = bf16[2,4,48,1152]{3,2,1,0:T(8,128)(2,1)S(1)} collective-permute-done((bf16[2,4,48,1152]{3,2,1,0:T(8,128)(2,1)S(1)}, bf16[2,4,48,1152]{3,2,1,0:T(8,128)(2,1)S(1)}, u32[]{:S(2)}, u32[]{:S(2)}) %collective-permute-start.42) | collective-permute-done | bytes 884768 | tf_op jit(solution)/shard_map/ppermute | solution.py:58
  309.1 1.9 fusion.11
  313.6 2.9 collective-permute-done.44.refs_3_
  320.0 5.1 %all-to-all-start.3 = ((bf16[32,4,1536]{2,1,0:T(4,128)(2,1)}), bf16[32,4,1536]{2,1,0:T(4,128)(2,1)S(1)}, u32[]{:S(2)}, u32[]{:S(2)}) async-start(bf16[32,4,1536]{2,1,0:T(4,128)(2,1)} %broadcast_in_dim.249), calls=%async_computation.3 | async-start | bytes 786432 | tf_op jit(solution)/shard_map/all_to_all | solution.py:896
  325.1 2.3 reshape.734
  327.4 2.7 fusion.64
  331.9 3.5 %collective-permute-start.49 = (bf16[48,1152]{1,0:T(8,128)(2,1)}, bf16[48,1152]{1,0:T(8,128)(2,1)}, u32[]{:S(2)}, u32[]{:S(2)}) collective-permute-start(bf16[48,1152]{1,0:T(8,128)(2,1)} %fusion.47), channel_id=1, source_target_pairs={{0,24},{1,25},{2,26},{3,27},{4,28},{5,29},{6,30},{7,31},{8,16},{9,... | collective-permute-start | bytes 331784 | tf_op jit(solution)/shard_map/ppermute | solution.py:58
  341.6 2.7 maximum_select_fusion.1
  (481 shorter events, 149.4 us)
Async XLA Ops:
  11.2 12.5 %collective-permute-start.2 = (bf16[256,768]{1,0:T(8,128)(2,1)}, bf16[256,768]{1,0:T(8,128)(2,1)S(1)}, u32[]{:S(2)}, u32[]{:S(2)}) collective-permute-start(bf16[256,768]{1,0:T(8,128)(2,1)} %get-tuple-element.238), channel_id=1, source_target_pairs={{0,1},{1,0},{2,3},{3,2},{4,5},{5,4},{6,7},{7,6},{8,9},{9,8},{10,11... | collective-permute-start | bytes 1179656 | tf_op jit(solution)/shard_map/ppermute | solution.py:52
  11.4 14.5 %collective-permute-start.1 = (bf16[48,1536]{1,0:T(8,128)(2,1)S(1)}, bf16[48,1536]{1,0:T(8,128)(2,1)S(1)}, u32[]{:S(2)}, u32[]{:S(2)}) collective-permute-start(bf16[48,1536]{1,0:T(8,128)(2,1)S(1)} %get-tuple-element.250), channel_id=1, source_target_pairs={{0,24},{1,25},{2,26},{3,27},{4,28},{5,29},{6,30},{7,31},{8,16},{9,... | collective-permute-start | bytes 442376 | tf_op jit(solution)/shard_map/ppermute | solution.py:58
  17.6 27.2 %all-to-all-start = ((bf16[32,26,256]{2,1,0:T(8,128)(2,1)}), bf16[32,26,256]{2,1,0:T(8,128)(2,1)S(1)}, u32[]{:S(2)}, u32[]{:S(2)}) async-start(bf16[32,26,256]{2,1,0:T(8,128)(2,1)} %copy.55), calls=%async_computation | async-start | bytes 1048576 | tf_op jit(solution)/shard_map/all_to_all | solution.py:761
  25.9 15.8 %collective-permute-start.3 = (bf16[2,48,1536]{2,1,0:T(8,128)(2,1)S(1)}, bf16[2,48,1536]{2,1,0:T(8,128)(2,1)S(1)}, u32[]{:S(2)}, u32[]{:S(2)}) collective-permute-start(bf16[2,48,1536]{2,1,0:T(8,128)(2,1)S(1)} %pad_maximum_fusion.6), channel_id=1, source_target_pairs={{0,8},{1,9},{2,10},{3,11},{4,12},{5,13},{6,14},{7,15},{8,0},{9,1},... | collective-permute-start | bytes 884744 | tf_op jit(solution)/shard_map/ppermute | solution.py:58
  28.5 28.6 %collective-permute-start.7 = (bf16[2,48,1536]{2,1,0:T(8,128)(2,1)}, bf16[2,48,1536]{2,1,0:T(8,128)(2,1)}, u32[]{:S(2)}, u32[]{:S(2)}) collective-permute-start(bf16[2,48,1536]{2,1,0:T(8,128)(2,1)} %pad_maximum_fusion.7), channel_id=1, source_target_pairs={{0,8},{1,9},{2,10},{3,11},{4,12},{5,13},{6,14},{7,15},{8,0},{9,1},... | collective-permute-start | bytes 884744 | tf_op jit(solution)/shard_map/ppermute | solution.py:58
  36.0 22.2 %collective-permute-start.6 = (bf16[48,1536]{1,0:T(8,128)(2,1)S(1)}, bf16[48,1536]{1,0:T(8,128)(2,1)S(1)}, u32[]{:S(2)}, u32[]{:S(2)}) collective-permute-start(bf16[48,1536]{1,0:T(8,128)(2,1)S(1)} %copy-done.73), channel_id=1, source_target_pairs={{0,24},{1,25},{2,26},{3,27},{4,28},{5,29},{6,30},{7,31},{8,16},{9,... | collective-permute-start | bytes 442376 | tf_op jit(solution)/shard_map/ppermute | solution.py:58
  41.8 24.2 %collective-permute-start.9 = (bf16[4,48,1536]{2,1,0:T(8,128)(2,1)S(1)}, bf16[4,48,1536]{2,1,0:T(8,128)(2,1)S(1)}, u32[]{:S(2)}, u32[]{:S(2)}) collective-permute-start(bf16[4,48,1536]{2,1,0:T(8,128)(2,1)S(1)} %pad_maximum_fusion.refs_0_), channel_id=1, source_target_pairs={{0,2},{1,5},{2,0},{3,7},{4,6},{5,1},{6,4},{7,3},{8,10},{9,13},{10,... | collective-permute-start | bytes 1769480 | tf_op jit(solution)/shard_map/ppermute | solution.py:58
  43.4 22.7 %collective-permute-start.10 = (bf16[4,48,1536]{2,1,0:T(8,128)(2,1)S(1)}, bf16[4,48,1536]{2,1,0:T(8,128)(2,1)}, u32[]{:S(2)}, u32[]{:S(2)}) collective-permute-start(bf16[4,48,1536]{2,1,0:T(8,128)(2,1)S(1)} %pad_maximum_fusion.refs_0_), channel_id=1, source_target_pairs={{0,4},{1,3},{2,6},{3,1},{4,0},{5,7},{6,2},{7,5},{8,12},{9,11},{10,... | collective-permute-start | bytes 1769480 | tf_op jit(solution)/shard_map/ppermute | solution.py:58
  53.3 11.8 %all-to-all-start.1 = ((f32[32,4,256]{2,1,0:T(4,128)}), f32[32,4,256]{2,1,0:T(4,128)}, u32[]{:S(2)}, u32[]{:S(2)}) async-start(f32[32,4,256]{2,1,0:T(4,128)} %copy.57), calls=%async_computation.1 | async-start | bytes 262144 | tf_op jit(solution)/shard_map/all_to_all | solution.py:781
  58.9 29.7 %collective-permute-start.8 = (bf16[2,48,1536]{2,1,0:T(8,128)(2,1)}, bf16[2,48,1536]{2,1,0:T(8,128)(2,1)}, u32[]{:S(2)}, u32[]{:S(2)}) collective-permute-start(bf16[2,48,1536]{2,1,0:T(8,128)(2,1)} %pad_maximum_fusion.8), channel_id=1, source_target_pairs={{0,8},{1,9},{2,10},{3,11},{4,12},{5,13},{6,14},{7,15},{8,0},{9,1},... | collective-permute-start | bytes 884744 | tf_op jit(solution)/shard_map/ppermute | solution.py:58
  60.7 32.7 %collective-permute-start.14 = (bf16[48,1536]{1,0:T(8,128)(2,1)S(1)}, bf16[48,1536]{1,0:T(8,128)(2,1)S(1)}, u32[]{:S(2)}, u32[]{:S(2)}) collective-permute-start(bf16[48,1536]{1,0:T(8,128)(2,1)S(1)} %bitcast.260), channel_id=1, source_target_pairs={{0,24},{1,25},{2,26},{3,27},{4,28},{5,29},{6,30},{7,31},{8,16},{9,... | collective-permute-start | bytes 442376 | tf_op jit(solution)/shard_map/ppermute | solution.py:58
  66.0 15.6 %collective-permute-start.13 = (bf16[4,48,1536]{2,1,0:T(8,128)(2,1)S(1)}, bf16[4,48,1536]{2,1,0:T(8,128)(2,1)S(1)}, u32[]{:S(2)}, u32[]{:S(2)}) collective-permute-start(bf16[4,48,1536]{2,1,0:T(8,128)(2,1)S(1)} %collective-permute-done.9.refs_1_), channel_id=1, source_target_pairs={{0,4},{1,3},{2,6},{3,1},{4,0},{5,7},{6,2},{7,5},{8,12},{9,11},{10,... | collective-permute-start | bytes 1769480 | tf_op jit(solution)/shard_map/ppermute | solution.py:58
  66.8 16.3 %collective-permute-start.11 = (bf16[4,48,1536]{2,1,0:T(8,128)(2,1)S(1)}, bf16[4,48,1536]{2,1,0:T(8,128)(2,1)S(1)}, u32[]{:S(2)}, u32[]{:S(2)}) collective-permute-start(bf16[4,48,1536]{2,1,0:T(8,128)(2,1)S(1)} %pad_maximum_fusion.1.refs_0_), channel_id=1, source_target_pairs={{0,2},{1,5},{2,0},{3,7},{4,6},{5,1},{6,4},{7,3},{8,10},{9,13},{10,... | collective-permute-start | bytes 1769480 | tf_op jit(solution)/shard_map/ppermute | solution.py:58
  68.4 19.5 %collective-permute-start.12 = (bf16[4,48,1536]{2,1,0:T(8,128)(2,1)S(1)}, bf16[4,48,1536]{2,1,0:T(8,128)(2,1)S(1)}, u32[]{:S(2)}, u32[]{:S(2)}) collective-permute-start(bf16[4,48,1536]{2,1,0:T(8,128)(2,1)S(1)} %pad_maximum_fusion.1.refs_0_), channel_id=1, source_target_pairs={{0,4},{1,3},{2,6},{3,1},{4,0},{5,7},{6,2},{7,5},{8,12},{9,11},{10,... | collective-permute-start | bytes 1769480 | tf_op jit(solution)/shard_map/ppermute | solution.py:58
  84.3 16.6 %collective-permute-start.15 = (bf16[768,1152]{1,0:T(8,128)(2,1)S(1)}, bf16[768,1152]{1,0:T(8,128)(2,1)S(1)}, u32[]{:S(2)}, u32[]{:S(2)}) collective-permute-start(bf16[768,1152]{1,0:T(8,128)(2,1)S(1)} %bitcast.241), channel_id=1, source_target_pairs={{0,1},{1,0},{2,3},{3,2},{4,5},{5,4},{6,7},{7,6},{8,9},{9,8},{10,11... | collective-permute-start | bytes 5308424 | tf_op jit(solution)/shard_map/ppermute | solution.py:52
  87.9 18.6 %collective-permute-start.16 = (bf16[4,48,1536]{2,1,0:T(8,128)(2,1)S(1)}, bf16[4,48,1536]{2,1,0:T(8,128)(2,1)S(1)}, u32[]{:S(2)}, u32[]{:S(2)}) collective-permute-start(bf16[4,48,1536]{2,1,0:T(8,128)(2,1)S(1)} %collective-permute-done.11.refs_1_), channel_id=1, source_target_pairs={{0,4},{1,3},{2,6},{3,1},{4,0},{5,7},{6,2},{7,5},{8,12},{9,11},{10,... | collective-permute-start | bytes 1769480 | tf_op jit(solution)/shard_map/ppermute | solution.py:58
  89.7 18.3 %collective-permute-start.17 = (bf16[4,48,1536]{2,1,0:T(8,128)(2,1)S(1)}, bf16[4,48,1536]{2,1,0:T(8,128)(2,1)S(1)}, u32[]{:S(2)}, u32[]{:S(2)}) collective-permute-start(bf16[4,48,1536]{2,1,0:T(8,128)(2,1)S(1)} %pad_maximum_fusion.2.refs_0_), channel_id=1, source_target_pairs={{0,2},{1,5},{2,0},{3,7},{4,6},{5,1},{6,4},{7,3},{8,10},{9,13},{10,... | collective-permute-start | bytes 1769480 | tf_op jit(solution)/shard_map/ppermute | solution.py:58
  91.0 19.4 %collective-permute-start.18 = (bf16[4,48,1536]{2,1,0:T(8,128)(2,1)S(1)}, bf16[4,48,1536]{2,1,0:T(8,128)(2,1)S(1)}, u32[]{:S(2)}, u32[]{:S(2)}) collective-permute-start(bf16[4,48,1536]{2,1,0:T(8,128)(2,1)S(1)} %pad_maximum_fusion.2.refs_0_), channel_id=1, source_target_pairs={{0,4},{1,3},{2,6},{3,1},{4,0},{5,7},{6,2},{7,5},{8,12},{9,11},{10,... | collective-permute-start | bytes 1769480 | tf_op jit(solution)/shard_map/ppermute | solution.py:58
  100.9 12.8 %collective-permute-start.19 = (bf16[768,384]{1,0:T(8,128)(2,1)S(1)}, bf16[768,384]{1,0:T(8,128)(2,1)S(1)}, u32[]{:S(2)}, u32[]{:S(2)}) collective-permute-start(bf16[768,384]{1,0:T(8,128)(2,1)S(1)} %bitcast.234), channel_id=1, source_target_pairs={{0,1},{1,0},{2,3},{3,2},{4,5},{5,4},{6,7},{7,6},{8,9},{9,8},{10,11... | collective-permute-start | bytes 1769480 | tf_op jit(solution)/shard_map/ppermute | solution.py:52
  110.5 18.2 %collective-permute-start.24 = (bf16[4,48,1536]{2,1,0:T(8,128)(2,1)S(1)}, bf16[4,48,1536]{2,1,0:T(8,128)(2,1)S(1)}, u32[]{:S(2)}, u32[]{:S(2)}) collective-permute-start(bf16[4,48,1536]{2,1,0:T(8,128)(2,1)S(1)} %pad_maximum_fusion.3.refs_0_), channel_id=1, source_target_pairs={{0,2},{1,5},{2,0},{3,7},{4,6},{5,1},{6,4},{7,3},{8,10},{9,13},{10,... | collective-permute-start | bytes 1769480 | tf_op jit(solution)/shard_map/ppermute | solution.py:58
  111.6 17.1 %collective-permute-start.25 = (bf16[4,48,1536]{2,1,0:T(8,128)(2,1)S(1)}, bf16[4,48,1536]{2,1,0:T(8,128)(2,1)S(1)}, u32[]{:S(2)}, u32[]{:S(2)}) collective-permute-start(bf16[4,48,1536]{2,1,0:T(8,128)(2,1)S(1)} %pad_maximum_fusion.3.refs_0_), channel_id=1, source_target_pairs={{0,4},{1,3},{2,6},{3,1},{4,0},{5,7},{6,2},{7,5},{8,12},{9,11},{10,... | collective-permute-start | bytes 1769480 | tf_op jit(solution)/shard_map/ppermute | solution.py:58
  112.4 19.9 %collective-permute-start.26 = (bf16[4,48,1536]{2,1,0:T(8,128)(2,1)S(1)}, bf16[4,48,1536]{2,1,0:T(8,128)(2,1)S(1)}, u32[]{:S(2)}, u32[]{:S(2)}) collective-permute-start(bf16[4,48,1536]{2,1,0:T(8,128)(2,1)S(1)} %collective-permute-done.17.refs_1_), channel_id=1, source_target_pairs={{0,4},{1,3},{2,6},{3,1},{4,0},{5,7},{6,2},{7,5},{8,12},{9,11},{10,... | collective-permute-start | bytes 1769480 | tf_op jit(solution)/shard_map/ppermute | solution.py:58
  116.4 13.2 %collective-permute-start.22 = (bf16[768,384]{1,0:T(8,128)(2,1)S(1)}, bf16[768,384]{1,0:T(8,128)(2,1)S(1)}, u32[]{:S(2)}, u32[]{:S(2)}) collective-permute-start(bf16[768,384]{1,0:T(8,128)(2,1)S(1)} %bitcast.237), channel_id=1, source_target_pairs={{0,1},{1,0},{2,3},{3,2},{4,5},{5,4},{6,7},{7,6},{8,9},{9,8},{10,11... | collective-permute-start | bytes 1769480 | tf_op jit(solution)/shard_map/ppermute | solution.py:52
  128.7 11.6 %collective-permute-start.27 = (bf16[4,48,1536]{2,1,0:T(8,128)(2,1)S(1)}, bf16[4,48,1536]{2,1,0:T(8,128)(2,1)S(1)}, u32[]{:S(2)}, u32[]{:S(2)}) collective-permute-start(bf16[4,48,1536]{2,1,0:T(8,128)(2,1)S(1)} %collective-permute-done.24.refs_1_), channel_id=1, source_target_pairs={{0,4},{1,3},{2,6},{3,1},{4,0},{5,7},{6,2},{7,5},{8,12},{9,11},{10,... | collective-permute-start | bytes 1769480 | tf_op jit(solution)/shard_map/ppermute | solution.py:58
  134.4 18.0 %collective-permute-start.28 = (bf16[768,1536]{1,0:T(8,128)(2,1)}, bf16[768,1536]{1,0:T(8,128)(2,1)}, u32[]{:S(2)}, u32[]{:S(2)}) collective-permute-start(bf16[768,1536]{1,0:T(8,128)(2,1)} %bitcast.46), channel_id=1, source_target_pairs={{0,1},{1,0},{2,3},{3,2},{4,5},{5,4},{6,7},{7,6},{8,9},{9,8},{10,11... | collective-permute-start | bytes 7077896 | tf_op jit(solution)/shard_map/ppermute | solution.py:52
  142.4 13.1 %collective-permute-start.29 = (bf16[768,1536]{1,0:T(8,128)(2,1)}, bf16[768,1536]{1,0:T(8,128)(2,1)}, u32[]{:S(2)}, u32[]{:S(2)}) collective-permute-start(bf16[768,1536]{1,0:T(8,128)(2,1)} %bitcast.47), channel_id=1, source_target_pairs={{0,1},{1,0},{2,3},{3,2},{4,5},{5,4},{6,7},{7,6},{8,9},{9,8},{10,11... | collective-permute-start | bytes 7077896 | tf_op jit(solution)/shard_map/ppermute | solution.py:52
  161.6 22.8 %collective-permute-start.31 = (bf16[768,1536]{1,0:T(8,128)(2,1)S(1)}, bf16[768,1536]{1,0:T(8,128)(2,1)S(1)}, u32[]{:S(2)}, u32[]{:S(2)}) collective-permute-start(bf16[768,1536]{1,0:T(8,128)(2,1)S(1)} %convolution_convert_fusion.4), channel_id=1, source_target_pairs={{0,1},{1,0},{2,3},{3,2},{4,5},{5,4},{6,7},{7,6},{8,9},{9,8},{10,11... | collective-permute-start | bytes 7077896 | tf_op jit(solution)/shard_map/ppermute | solution.py:52
  167.7 18.2 %collective-permute-start.32 = (bf16[768,1536]{1,0:T(8,128)(2,1)S(1)}, bf16[768,1536]{1,0:T(8,128)(2,1)S(1)}, u32[]{:S(2)}, u32[]{:S(2)}) collective-permute-start(bf16[768,1536]{1,0:T(8,128)(2,1)S(1)} %convolution_convert_fusion.3), channel_id=1, source_target_pairs={{0,1},{1,0},{2,3},{3,2},{4,5},{5,4},{6,7},{7,6},{8,9},{9,8},{10,11... | collective-permute-start | bytes 7077896 | tf_op jit(solution)/shard_map/ppermute | solution.py:52
  168.1 15.1 %collective-permute-start.30 = (f32[256,768]{1,0:T(8,128)S(1)}, f32[256,768]{1,0:T(8,128)S(1)}, u32[]{:S(2)}, u32[]{:S(2)}) collective-permute-start(f32[256,768]{1,0:T(8,128)S(1)} %get-tuple-element.165), channel_id=1, source_target_pairs={{0,1},{1,0},{2,3},{3,2},{4,5},{5,4},{6,7},{7,6},{8,9},{9,8},{10,11... | collective-permute-start | bytes 2359304 | tf_op jit(solution)/shard_map/ppermute | solution.py:52
  182.1 37.4 %collective-permute-start.34 = (bf16[768,384]{1,0:T(8,128)(2,1)}, bf16[768,384]{1,0:T(8,128)(2,1)}, u32[]{:S(2)}, u32[]{:S(2)}) collective-permute-start(bf16[768,384]{1,0:T(8,128)(2,1)} %convolution_convert_fusion.12), channel_id=1, source_target_pairs={{0,1},{1,0},{2,3},{3,2},{4,5},{5,4},{6,7},{7,6},{8,9},{9,8},{10,11... | collective-permute-start | bytes 1769480 | tf_op jit(solution)/shard_map/ppermute | solution.py:52
  191.6 34.1 %collective-permute-start.33 = (bf16[2,4,48,3072]{3,2,1,0:T(8,128)(2,1)}, bf16[2,4,48,3072]{3,2,1,0:T(8,128)(2,1)}, u32[]{:S(2)}, u32[]{:S(2)}) collective-permute-start(bf16[2,4,48,3072]{3,2,1,0:T(8,128)(2,1)} %add_blocks.6), channel_id=1, source_target_pairs={{0,2},{1,5},{2,0},{3,7},{4,6},{5,1},{6,4},{7,3},{8,10},{9,13},{10,... | collective-permute-start | bytes 7077896 | tf_op jit(solution)/shard_map/ppermute | solution.py:58
  210.9 11.8 %collective-permute-start.36 = (bf16[768,768]{1,0:T(8,128)(2,1)}, bf16[768,768]{1,0:T(8,128)(2,1)}, u32[]{:S(2)}, u32[]{:S(2)}) collective-permute-start(bf16[768,768]{1,0:T(8,128)(2,1)} %fusion.23), channel_id=1, source_target_pairs={{0,1},{1,0},{2,3},{3,2},{4,5},{5,4},{6,7},{7,6},{8,9},{9,8},{10,11... | collective-permute-start | bytes 3538952 | tf_op jit(solution)/shard_map/ppermute | solution.py:52
  228.8 24.5 %collective-permute-start.37 = (bf16[1,4,48,3072]{3,2,1,0:T(8,128)(2,1)}, bf16[1,4,48,3072]{3,2,1,0:T(8,128)(2,1)}, u32[]{:S(2)}, u32[]{:S(2)}) collective-permute-start(bf16[1,4,48,3072]{3,2,1,0:T(8,128)(2,1)} %add_blocks.7), channel_id=1, source_target_pairs={{0,4},{1,3},{2,6},{3,1},{4,0},{5,7},{6,2},{7,5},{8,12},{9,11},{10,... | collective-permute-start | bytes 3538952 | tf_op jit(solution)/shard_map/ppermute | solution.py:58
  240.8 29.3 %collective-permute-start.40 = (bf16[2,4,48,1920]{3,2,1,0:T(8,128)(2,1)}, bf16[2,4,48,1920]{3,2,1,0:T(8,128)(2,1)}, u32[]{:S(2)}, u32[]{:S(2)}) collective-permute-start(bf16[2,4,48,1920]{3,2,1,0:T(8,128)(2,1)} %add_blocks.8), channel_id=1, source_target_pairs={{0,2},{1,5},{2,0},{3,7},{4,6},{5,1},{6,4},{7,3},{8,10},{9,13},{10,... | collective-permute-start | bytes 4423688 | tf_op jit(solution)/shard_map/ppermute | solution.py:58
  248.6 71.4 %all-to-all-start.2 = ((bf16[16,4,5376]{2,1,0:T(4,128)(2,1)}), bf16[16,4,5376]{2,1,0:T(4,128)(2,1)}, u32[]{:S(2)}, u32[]{:S(2)}) async-start(bf16[16,4,5376]{2,1,0:T(4,128)(2,1)} %broadcast_in_dim.244), calls=%async_computation.2 | async-start | bytes 1376256 | tf_op jit(solution)/shard_map/all_to_all | solution.py:896
  253.3 55.8 %collective-permute-start.48 = (bf16[4,128,768]{2,1,0:T(8,128)(2,1)}, bf16[4,128,768]{2,1,0:T(8,128)(2,1)S(1)}, u32[]{:S(2)}, u32[]{:S(2)}) collective-permute-start(bf16[4,128,768]{2,1,0:T(8,128)(2,1)} %get-tuple-element.234), channel_id=1, source_target_pairs={{0,1},{1,0},{2,3},{3,2},{4,5},{5,4},{6,7},{7,6},{8,9},{9,8},{10,11... | collective-permute-start | bytes 2359304 | tf_op jit(solution)/shard_map/ppermute | solution.py:52
  258.1 21.1 %collective-permute-start.39 = (bf16[2,48,3072]{2,1,0:T(8,128)(2,1)S(1)}, bf16[2,48,3072]{2,1,0:T(8,128)(2,1)S(1)}, u32[]{:S(2)}, u32[]{:S(2)}) collective-permute-start(bf16[2,48,3072]{2,1,0:T(8,128)(2,1)S(1)} %get-tuple-element.195), channel_id=1, source_target_pairs={{0,8},{1,9},{2,10},{3,11},{4,12},{5,13},{6,14},{7,15},{8,0},{9,1},... | collective-permute-start | bytes 1769480 | tf_op jit(solution)/shard_map/ppermute | solution.py:58
  271.6 27.2 %collective-permute-start.43 = (bf16[1,4,48,1920]{3,2,1,0:T(8,128)(2,1)S(1)}, bf16[1,4,48,1920]{3,2,1,0:T(8,128)(2,1)S(1)}, u32[]{:S(2)}, u32[]{:S(2)}) collective-permute-start(bf16[1,4,48,1920]{3,2,1,0:T(8,128)(2,1)S(1)} %add_blocks.9), channel_id=1, source_target_pairs={{0,4},{1,3},{2,6},{3,1},{4,0},{5,7},{6,2},{7,5},{8,12},{9,11},{10,... | collective-permute-start | bytes 2211848 | tf_op jit(solution)/shard_map/ppermute | solution.py:58
  274.3 19.2 %collective-permute-start.41 = (bf16[768,1152]{1,0:T(8,128)(2,1)S(1)}, bf16[768,1152]{1,0:T(8,128)(2,1)S(1)}, u32[]{:S(2)}, u32[]{:S(2)}) collective-permute-start(bf16[768,1152]{1,0:T(8,128)(2,1)S(1)} %convolution_convert_fusion.2), channel_id=1, source_target_pairs={{0,1},{1,0},{2,3},{3,2},{4,5},{5,4},{6,7},{7,6},{8,9},{9,8},{10,11... | collective-permute-start | bytes 5308424 | tf_op jit(solution)/shard_map/ppermute | solution.py:52
  279.2 21.7 %collective-permute-start.56 = (bf16[48,3072]{1,0:T(8,128)(2,1)S(1)}, bf16[48,3072]{1,0:T(8,128)(2,1)S(1)}, u32[]{:S(2)}, u32[]{:S(2)}) collective-permute-start(bf16[48,3072]{1,0:T(8,128)(2,1)S(1)} %fusion.40), channel_id=1, source_target_pairs={{0,24},{1,25},{2,26},{3,27},{4,28},{5,29},{6,30},{7,31},{8,16},{9,... | collective-permute-start | bytes 884744 | tf_op jit(solution)/shard_map/ppermute | solution.py:58
  294.8 13.1 %collective-permute-start.42 = (bf16[2,4,48,1152]{3,2,1,0:T(8,128)(2,1)S(1)}, bf16[2,4,48,1152]{3,2,1,0:T(8,128)(2,1)S(1)}, u32[]{:S(2)}, u32[]{:S(2)}) collective-permute-start(bf16[2,4,48,1152]{3,2,1,0:T(8,128)(2,1)S(1)} %add_blocks.10), channel_id=1, source_target_pairs={{0,2},{1,5},{2,0},{3,7},{4,6},{5,1},{6,4},{7,3},{8,10},{9,13},{10,... | collective-permute-start | bytes 2654216 | tf_op jit(solution)/shard_map/ppermute | solution.py:58
  300.8 17.5 %collective-permute-start.46 = (bf16[2,48,1920]{2,1,0:T(8,128)(2,1)S(1)}, bf16[2,48,1920]{2,1,0:T(8,128)(2,1)S(1)}, u32[]{:S(2)}, u32[]{:S(2)}) collective-permute-start(bf16[2,48,1920]{2,1,0:T(8,128)(2,1)S(1)} %get-tuple-element.204), channel_id=1, source_target_pairs={{0,8},{1,9},{2,10},{3,11},{4,12},{5,13},{6,14},{7,15},{8,0},{9,1},... | collective-permute-start | bytes 1105928 | tf_op jit(solution)/shard_map/ppermute | solution.py:58
  313.4 28.2 %collective-permute-start.47 = (f32[256,768]{1,0:T(8,128)S(1)}, f32[256,768]{1,0:T(8,128)}, u32[]{:S(2)}, u32[]{:S(2)}) collective-permute-start(f32[256,768]{1,0:T(8,128)S(1)} %get-tuple-element.218), channel_id=1, source_target_pairs={{0,1},{1,0},{2,3},{3,2},{4,5},{5,4},{6,7},{7,6},{8,9},{9,8},{10,11... | collective-permute-start | bytes 2359304 | tf_op jit(solution)/shard_map/ppermute | solution.py:52
  318.3 12.1 %collective-permute-start.45 = (bf16[2,48,1152]{2,1,0:T(8,128)(2,1)S(1)}, bf16[2,48,1152]{2,1,0:T(8,128)(2,1)}, u32[]{:S(2)}, u32[]{:S(2)}) collective-permute-start(bf16[2,48,1152]{2,1,0:T(8,128)(2,1)S(1)} %get-tuple-element.212), channel_id=1, source_target_pairs={{0,8},{1,9},{2,10},{3,11},{4,12},{5,13},{6,14},{7,15},{8,0},{9,1},... | collective-permute-start | bytes 663560 | tf_op jit(solution)/shard_map/ppermute | solution.py:58
  319.2 16.3 %collective-permute-start.52 = (bf16[48,1920]{1,0:T(8,128)(2,1)}, bf16[48,1920]{1,0:T(8,128)(2,1)S(1)}, u32[]{:S(2)}, u32[]{:S(2)}) collective-permute-start(bf16[48,1920]{1,0:T(8,128)(2,1)} %fusion.46), channel_id=1, source_target_pairs={{0,24},{1,25},{2,26},{3,27},{4,28},{5,29},{6,30},{7,31},{8,16},{9,... | collective-permute-start | bytes 552968 | tf_op jit(solution)/shard_map/ppermute | solution.py:58
  320.0 20.1 %all-to-all-start.3 = ((bf16[32,4,1536]{2,1,0:T(4,128)(2,1)}), bf16[32,4,1536]{2,1,0:T(4,128)(2,1)S(1)}, u32[]{:S(2)}, u32[]{:S(2)}) async-start(bf16[32,4,1536]{2,1,0:T(4,128)(2,1)} %broadcast_in_dim.249), calls=%async_computation.3 | async-start | bytes 786432 | tf_op jit(solution)/shard_map/all_to_all | solution.py:896
  330.1 14.2 %collective-permute-start.50 = (f32[25,5376]{1,0:T(8,128)}, f32[25,5376]{1,0:T(8,128)}, u32[]{:S(2)}, u32[]{:S(2)}) collective-permute-start(f32[25,5376]{1,0:T(8,128)} %fusion.64), channel_id=1, source_target_pairs={{0,1},{1,0},{2,3},{3,2},{4,5},{5,4},{6,7},{7,6},{8,9},{9,8},{10,11... | collective-permute-start | bytes 1612808 | tf_op jit(solution)/shard_map/ppermute | solution.py:52
  331.9 15.8 %collective-permute-start.49 = (bf16[48,1152]{1,0:T(8,128)(2,1)}, bf16[48,1152]{1,0:T(8,128)(2,1)}, u32[]{:S(2)}, u32[]{:S(2)}) collective-permute-start(bf16[48,1152]{1,0:T(8,128)(2,1)} %fusion.47), channel_id=1, source_target_pairs={{0,24},{1,25},{2,26},{3,27},{4,28},{5,29},{6,30},{7,31},{8,16},{9,... | collective-permute-start | bytes 331784 | tf_op jit(solution)/shard_map/ppermute | solution.py:58
  (119 other events, 746.7 us)
